TPU v7x, 32 devices: a whole 2x2x4 slice. The times are simulated.
32 devices in a mesh: grp: 2 (over y), lat: 4 (over z), ch: 2 (over x), lon: 2 (over core).
Axes of the slice: x: 2, y: 2, z: 4, core: 2. Of those that a mesh axis runs over, the one named last changes fastest.
Arguments:
- grad_out: bfloat16 [384, 16, 1024], P('ch', ('grp', 'lat'), 'lon'), parts along dimension 1, may hold values from -6 to 6
- saved_basis: bfloat16 [9, 384, 16, 1024], P(None, 'ch', ('grp', 'lat'), 'lon'), parts along dimension 2, may hold values from -6 to 6
- weight: bfloat16 [384, 9, 384], P(None, None, 'ch'), may hold values from -0.109375 to 0.109375
- quad_tiles: bfloat16 [8, 16, 9, 64, 64], P('lat'), may hold values from -0.25 to 0.25
- col_rows: int32 [8, 16], P('lat'), may hold values from 0 to 7, as said below
- col_shift: int32 [8, 16], P('lat'), may hold values from 0 to 15
- block_count: int32 [8], P('lat'), may hold values from 2 to 16, as said below
Outputs:
- grad_input: float32 [384, 16, 1024], P('ch', ('grp', 'lat'), 'lon'), parts along dimension 1
- grad_weight: float32 [768, 9, 384], P(('grp', 'lat', 'lon'), None, 'ch'), parts along dimension 0
There are 2 independent parts, one for each index of `grp`. A program takes and returns all parts, laid end to end along the dimension named above; an argument that names none is the same for every part. Nothing has to cross between parts.
Inputs may be any that keep to these rules, and one draw needn't show every extreme that they name: `col_rows`: each entry's input row lies within 4 rows of its own row. `block_count`: entries at or past a row's count are not used.
All inputs are finite; a program needn't handle non-finite values.
Results may differ from a plain program's by a relative error of at most 0.0029.
Values may be sent and summed in bfloat16 or wider, within the bound.
A program may use at most 128 MiB of HBM per device.

v0:
```python
import jax
import jax.numpy as jnp
from jax import lax
from jax.sharding import PartitionSpec as P

HALO_DEV = 2


def passed_along(value, axis, steps):
    count = lax.axis_size(axis)
    initial, last = (max(0, -steps), min(count, count - steps))
    return lax.ppermute(value, axis, [(source, source + steps) for source in range(initial, last)])


def body(grad_out, saved_basis, weight, quad_tiles, col_rows, col_shift, block_count):
    channels, row_count, width_local = grad_out.shape
    basis_count = saved_basis.shape[0]
    out_channels = weight.shape[0]
    entries = quad_tiles.shape[1]
    blocks = width_local // 64
    reach_dev = HALO_DEV
    lat_devices = lax.axis_size("lat")
    lon_devices = lax.axis_size("lon")
    cycle_len = width_local * lon_devices
    points = row_count * width_local
    window = (2 * reach_dev + 1) * row_count
    full_out = lax.all_gather(grad_out, "ch", axis=0, tiled=True).reshape(out_channels, points)
    flat_basis = saved_basis.reshape(basis_count * channels, points)
    own_rows = out_channels // (lat_devices * lon_devices)
    product = lax.dot_general(
        full_out, flat_basis, (((1,), (1,)), ((), ())), preferred_element_type=jnp.float32
    )
    grad_weight = lax.psum_scatter(
        product.reshape(own_rows * lax.axis_size(("lat", "lon")), basis_count, channels),
        ("lat", "lon"),
        scatter_dimension=0,
        tiled=True,
    )
    mixing = weight.reshape(out_channels, basis_count * channels)
    mixed_grad = lax.dot_general(
        mixing, full_out, (((0,), (0,)), ((), ())), preferred_element_type=jnp.float32
    ).astype(jnp.bfloat16)
    mixed_grad = mixed_grad.reshape(basis_count, channels, row_count, blocks, 64)
    pieces = jnp.einsum(
        "kcrjp,rekpq->recjq", mixed_grad, quad_tiles, preferred_element_type=jnp.float32
    )
    pieces = pieces.reshape(row_count, entries, channels, width_local)
    lat_index = lax.axis_index("lat")
    lon_index = lax.axis_index("lon")
    window_start = lat_index * row_count - reach_dev * row_count
    targets = col_rows - window_start
    starts = (lon_index * width_local + col_shift * 64) % cycle_len
    live_weight = (jnp.arange(entries, dtype=jnp.int32)[None, :] < block_count[:, None]).astype(
        jnp.float32
    )
    zero_int = jnp.zeros((), jnp.int32)

    def place_entry(entry_id, summed):
        entry_pieces = lax.dynamic_index_in_dim(pieces, entry_id, 1, keepdims=False)
        entry_targets = lax.dynamic_index_in_dim(targets, entry_id, 1, keepdims=False)
        entry_starts = lax.dynamic_index_in_dim(starts, entry_id, 1, keepdims=False)
        entry_live = lax.dynamic_index_in_dim(live_weight, entry_id, 1, keepdims=False)
        for row in range(row_count):
            doubled = jnp.zeros((channels, 2 * cycle_len), jnp.float32)
            doubled = lax.dynamic_update_slice(
                doubled, entry_pieces[row] * entry_live[row], (zero_int, entry_starts[row])
            )
            rolled = doubled[:, :cycle_len] + doubled[:, cycle_len:]
            current = lax.dynamic_index_in_dim(summed, entry_targets[row], 1, keepdims=False)
            summed = lax.dynamic_update_index_in_dim(
                summed, current + rolled, entry_targets[row], 1
            )
        return summed

    placed = lax.fori_loop(
        0, entries, place_entry, jnp.zeros((channels, window, cycle_len), jnp.float32)
    )
    placed = placed.reshape(channels, 2 * reach_dev + 1, row_count, cycle_len)
    offsets = [step for step in range(-reach_dev, reach_dev + 1) if step != 0]
    halves = lax.psum_scatter(placed, "lon", scatter_dimension=3, tiled=True)
    summed = halves[:, reach_dev]
    for offset in offsets:
        summed = summed + passed_along(halves[:, reach_dev + offset], "lat", offset)
    return (summed, grad_weight)


def solution(mesh):
    in_specs = (
        P("ch", ("grp", "lat"), "lon"),
        P(None, "ch", ("grp", "lat"), "lon"),
        P(None, None, "ch"),
        P("lat", None, None, None, None),
        P("lat", None),
        P("lat", None),
        P("lat"),
    )
    out_specs = (P("ch", ("grp", "lat"), "lon"), P(("grp", "lat", "lon"), None, "ch"))
    return jax.shard_map(body, mesh=mesh, in_specs=in_specs, out_specs=out_specs, check_vma=False)
```

profile of v0, /device:TPU:0, one launch (start us, length us, event | category | flops | bytes accessed | tf_op | source)
XLA Modules:
  0.0 1329.3 jit_solution(3906829867553185087)
XLA Ops:
  38.8 18.6 %fusion.7 = f32[2,16,192,8,64]{2,4,1,3,0:T(8,128)} fusion(bf16[9,192,2,8,64,1]{4,3,2,1,0,5:T(8,128)(2,1)} %bitcast.79, bf16[2,16,9,64,64]{4,3,2,1,0:T(8,128)(2,1)} %param.12), kind=kOutput, calls=%fused_computation.16 | convolution fusion | flops 3623878656 | bytes 18481152 | tf_op jit(solution)/shard_map/kcrjp,rekpq->recjq/dot_general | solution.py:44
  69.0 16.5 %copy.20 = f32[2,16,192,512]{3,2,1,0:T(8,128)} copy(f32[2,16,192,512]{2,3,1,0:T(8,128)} %bitcast.77) | data formatting | bytes 25165824 | tf_op jit(solution)/shard_map/while | solution.py:75
  92.4 1109.0 %while.13 = (s32[]{:T(128)}, f32[192,10,1024]{2,1,0:T(8,128)}, s32[2,16]{1,0:T(2,128)S(1)}, f32[2,16,192,512]{3,2,1,0:T(8,128)}, f32[2,16]{1,0:T(2,128)S(1)}, /*...) while((s32[]{:T(128)}, f32[192,10,1024]{2,1,0:T(8,128)}, ...), condition=%wide.region_1.2_spmd, body=%wide.region_0.0_spmd.sunk | while | flops 983055 | bytes 22020512 | solution.py:75
  113.2 15.9 %dynamic_update_slice.34 = f32[192,10,1024]{2,1,0:T(8,128)} dynamic-update-slice(f32[192,10,1024]{2,1,0:T(8,128)} %get-tuple-element.218, f32[192,1,1024]{2,1,0:T(1,128)} %copy.49, s32[]{:T(128)} %constant.89.clone.1..sunk, s32[]{:T(128)S(6)} %select_n.57, s32[]{:T(128)} %constant.89.clone.1..sunk) | dynamic-update-slice | bytes 1572868 | tf_op jit(solution)/shard_map/while/body/eval_jaxpr/jit(dynamic_update_index_in_dim)/dynamic_update_slice | solution.py:70
  145.9 15.9 %dynamic_update_slice.36 = f32[192,10,1024]{2,1,0:T(8,128)} dynamic-update-slice(f32[192,10,1024]{2,1,0:T(8,128)} %dynamic_update_slice.34, f32[192,1,1024]{2,1,0:T(1,128)} %broadcast_in_dim.22, s32[]{:T(128)} %constant.89.clone.1..sunk, s32[]{:T(128)S(6)} %select_n.59, s32[]{:T(128)} %constant.89.clone.1..sunk) | dynamic-update-slice | bytes 1572868 | tf_op jit(solution)/shard_map/while/body/eval_jaxpr/jit(dynamic_update_index_in_dim)/dynamic_update_slice | solution.py:70
  252.1 15.9 %dynamic_update_slice.34 = f32[192,10,1024]{2,1,0:T(8,128)} dynamic-update-slice(f32[192,10,1024]{2,1,0:T(8,128)} %get-tuple-element.218, f32[192,1,1024]{2,1,0:T(1,128)} %copy.49, s32[]{:T(128)} %constant.89.clone.1..sunk, s32[]{:T(128)S(6)} %select_n.57, s32[]{:T(128)} %constant.89.clone.1..sunk) | dynamic-update-slice | bytes 1572868 | tf_op jit(solution)/shard_map/while/body/eval_jaxpr/jit(dynamic_update_index_in_dim)/dynamic_update_slice | solution.py:70
  284.5 15.9 %dynamic_update_slice.36 = f32[192,10,1024]{2,1,0:T(8,128)} dynamic-update-slice(f32[192,10,1024]{2,1,0:T(8,128)} %dynamic_update_slice.34, f32[192,1,1024]{2,1,0:T(1,128)} %broadcast_in_dim.22, s32[]{:T(128)} %constant.89.clone.1..sunk, s32[]{:T(128)S(6)} %select_n.59, s32[]{:T(128)} %constant.89.clone.1..sunk) | dynamic-update-slice | bytes 1572868 | tf_op jit(solution)/shard_map/while/body/eval_jaxpr/jit(dynamic_update_index_in_dim)/dynamic_update_slice | solution.py:70
  321.3 15.9 %dynamic_update_slice.34 = f32[192,10,1024]{2,1,0:T(8,128)} dynamic-update-slice(f32[192,10,1024]{2,1,0:T(8,128)} %get-tuple-element.218, f32[192,1,1024]{2,1,0:T(1,128)} %copy.49, s32[]{:T(128)} %constant.89.clone.1..sunk, s32[]{:T(128)S(6)} %select_n.57, s32[]{:T(128)} %constant.89.clone.1..sunk) | dynamic-update-slice | bytes 1572868 | tf_op jit(solution)/shard_map/while/body/eval_jaxpr/jit(dynamic_update_index_in_dim)/dynamic_update_slice | solution.py:70
  390.7 15.9 %dynamic_update_slice.34 = f32[192,10,1024]{2,1,0:T(8,128)} dynamic-update-slice(f32[192,10,1024]{2,1,0:T(8,128)} %get-tuple-element.218, f32[192,1,1024]{2,1,0:T(1,128)} %copy.49, s32[]{:T(128)} %constant.89.clone.1..sunk, s32[]{:T(128)S(6)} %select_n.57, s32[]{:T(128)} %constant.89.clone.1..sunk) | dynamic-update-slice | bytes 1572868 | tf_op jit(solution)/shard_map/while/body/eval_jaxpr/jit(dynamic_update_index_in_dim)/dynamic_update_slice | solution.py:70
  423.1 15.9 %dynamic_update_slice.36 = f32[192,10,1024]{2,1,0:T(8,128)} dynamic-update-slice(f32[192,10,1024]{2,1,0:T(8,128)} %dynamic_update_slice.34, f32[192,1,1024]{2,1,0:T(1,128)} %broadcast_in_dim.22, s32[]{:T(128)} %constant.89.clone.1..sunk, s32[]{:T(128)S(6)} %select_n.59, s32[]{:T(128)} %constant.89.clone.1..sunk) | dynamic-update-slice | bytes 1572868 | tf_op jit(solution)/shard_map/while/body/eval_jaxpr/jit(dynamic_update_index_in_dim)/dynamic_update_slice | solution.py:70
  459.9 15.9 %dynamic_update_slice.34 = f32[192,10,1024]{2,1,0:T(8,128)} dynamic-update-slice(f32[192,10,1024]{2,1,0:T(8,128)} %get-tuple-element.218, f32[192,1,1024]{2,1,0:T(1,128)} %copy.49, s32[]{:T(128)} %constant.89.clone.1..sunk, s32[]{:T(128)S(6)} %select_n.57, s32[]{:T(128)} %constant.89.clone.1..sunk) | dynamic-update-slice | bytes 1572868 | tf_op jit(solution)/shard_map/while/body/eval_jaxpr/jit(dynamic_update_index_in_dim)/dynamic_update_slice | solution.py:70
  492.2 15.9 %dynamic_update_slice.36 = f32[192,10,1024]{2,1,0:T(8,128)} dynamic-update-slice(f32[192,10,1024]{2,1,0:T(8,128)} %dynamic_update_slice.34, f32[192,1,1024]{2,1,0:T(1,128)} %broadcast_in_dim.22, s32[]{:T(128)} %constant.89.clone.1..sunk, s32[]{:T(128)S(6)} %select_n.59, s32[]{:T(128)} %constant.89.clone.1..sunk) | dynamic-update-slice | bytes 1572868 | tf_op jit(solution)/shard_map/while/body/eval_jaxpr/jit(dynamic_update_index_in_dim)/dynamic_update_slice | solution.py:70
  561.4 15.9 %dynamic_update_slice.36 = f32[192,10,1024]{2,1,0:T(8,128)} dynamic-update-slice(f32[192,10,1024]{2,1,0:T(8,128)} %dynamic_update_slice.34, f32[192,1,1024]{2,1,0:T(1,128)} %broadcast_in_dim.22, s32[]{:T(128)} %constant.89.clone.1..sunk, s32[]{:T(128)S(6)} %select_n.59, s32[]{:T(128)} %constant.89.clone.1..sunk) | dynamic-update-slice | bytes 1572868 | tf_op jit(solution)/shard_map/while/body/eval_jaxpr/jit(dynamic_update_index_in_dim)/dynamic_update_slice | solution.py:70
  598.2 15.9 %dynamic_update_slice.34 = f32[192,10,1024]{2,1,0:T(8,128)} dynamic-update-slice(f32[192,10,1024]{2,1,0:T(8,128)} %get-tuple-element.218, f32[192,1,1024]{2,1,0:T(1,128)} %copy.49, s32[]{:T(128)} %constant.89.clone.1..sunk, s32[]{:T(128)S(6)} %select_n.57, s32[]{:T(128)} %constant.89.clone.1..sunk) | dynamic-update-slice | bytes 1572868 | tf_op jit(solution)/shard_map/while/body/eval_jaxpr/jit(dynamic_update_index_in_dim)/dynamic_update_slice | solution.py:70
  630.8 15.9 %dynamic_update_slice.36 = f32[192,10,1024]{2,1,0:T(8,128)} dynamic-update-slice(f32[192,10,1024]{2,1,0:T(8,128)} %dynamic_update_slice.34, f32[192,1,1024]{2,1,0:T(1,128)} %broadcast_in_dim.22, s32[]{:T(128)} %constant.89.clone.1..sunk, s32[]{:T(128)S(6)} %select_n.59, s32[]{:T(128)} %constant.89.clone.1..sunk) | dynamic-update-slice | bytes 1572868 | tf_op jit(solution)/shard_map/while/body/eval_jaxpr/jit(dynamic_update_index_in_dim)/dynamic_update_slice | solution.py:70
  667.6 15.9 %dynamic_update_slice.34 = f32[192,10,1024]{2,1,0:T(8,128)} dynamic-update-slice(f32[192,10,1024]{2,1,0:T(8,128)} %get-tuple-element.218, f32[192,1,1024]{2,1,0:T(1,128)} %copy.49, s32[]{:T(128)} %constant.89.clone.1..sunk, s32[]{:T(128)S(6)} %select_n.57, s32[]{:T(128)} %constant.89.clone.1..sunk) | dynamic-update-slice | bytes 1572868 | tf_op jit(solution)/shard_map/while/body/eval_jaxpr/jit(dynamic_update_index_in_dim)/dynamic_update_slice | solution.py:70
  737.0 15.9 %dynamic_update_slice.34 = f32[192,10,1024]{2,1,0:T(8,128)} dynamic-update-slice(f32[192,10,1024]{2,1,0:T(8,128)} %get-tuple-element.218, f32[192,1,1024]{2,1,0:T(1,128)} %copy.49, s32[]{:T(128)} %constant.89.clone.1..sunk, s32[]{:T(128)S(6)} %select_n.57, s32[]{:T(128)} %constant.89.clone.1..sunk) | dynamic-update-slice | bytes 1572868 | tf_op jit(solution)/shard_map/while/body/eval_jaxpr/jit(dynamic_update_index_in_dim)/dynamic_update_slice | solution.py:70
  769.4 15.9 %dynamic_update_slice.36 = f32[192,10,1024]{2,1,0:T(8,128)} dynamic-update-slice(f32[192,10,1024]{2,1,0:T(8,128)} %dynamic_update_slice.34, f32[192,1,1024]{2,1,0:T(1,128)} %broadcast_in_dim.22, s32[]{:T(128)} %constant.89.clone.1..sunk, s32[]{:T(128)S(6)} %select_n.59, s32[]{:T(128)} %constant.89.clone.1..sunk) | dynamic-update-slice | bytes 1572868 | tf_op jit(solution)/shard_map/while/body/eval_jaxpr/jit(dynamic_update_index_in_dim)/dynamic_update_slice | solution.py:70
  875.6 15.9 %dynamic_update_slice.34 = f32[192,10,1024]{2,1,0:T(8,128)} dynamic-update-slice(f32[192,10,1024]{2,1,0:T(8,128)} %get-tuple-element.218, f32[192,1,1024]{2,1,0:T(1,128)} %copy.49, s32[]{:T(128)} %constant.89.clone.1..sunk, s32[]{:T(128)S(6)} %select_n.57, s32[]{:T(128)} %constant.89.clone.1..sunk) | dynamic-update-slice | bytes 1572868 | tf_op jit(solution)/shard_map/while/body/eval_jaxpr/jit(dynamic_update_index_in_dim)/dynamic_update_slice | solution.py:70
  908.0 15.9 %dynamic_update_slice.36 = f32[192,10,1024]{2,1,0:T(8,128)} dynamic-update-slice(f32[192,10,1024]{2,1,0:T(8,128)} %dynamic_update_slice.34, f32[192,1,1024]{2,1,0:T(1,128)} %broadcast_in_dim.22, s32[]{:T(128)} %constant.89.clone.1..sunk, s32[]{:T(128)S(6)} %select_n.59, s32[]{:T(128)} %constant.89.clone.1..sunk) | dynamic-update-slice | bytes 1572868 | tf_op jit(solution)/shard_map/while/body/eval_jaxpr/jit(dynamic_update_index_in_dim)/dynamic_update_slice | solution.py:70
  944.8 15.9 %dynamic_update_slice.34 = f32[192,10,1024]{2,1,0:T(8,128)} dynamic-update-slice(f32[192,10,1024]{2,1,0:T(8,128)} %get-tuple-element.218, f32[192,1,1024]{2,1,0:T(1,128)} %copy.49, s32[]{:T(128)} %constant.89.clone.1..sunk, s32[]{:T(128)S(6)} %select_n.57, s32[]{:T(128)} %constant.89.clone.1..sunk) | dynamic-update-slice | bytes 1572868 | tf_op jit(solution)/shard_map/while/body/eval_jaxpr/jit(dynamic_update_index_in_dim)/dynamic_update_slice | solution.py:70
  1152.8 15.9 %dynamic_update_slice.34 = f32[192,10,1024]{2,1,0:T(8,128)} dynamic-update-slice(f32[192,10,1024]{2,1,0:T(8,128)} %get-tuple-element.218, f32[192,1,1024]{2,1,0:T(1,128)} %copy.49, s32[]{:T(128)} %constant.89.clone.1..sunk, s32[]{:T(128)S(6)} %select_n.57, s32[]{:T(128)} %constant.89.clone.1..sunk) | dynamic-update-slice | bytes 1572868 | tf_op jit(solution)/shard_map/while/body/eval_jaxpr/jit(dynamic_update_index_in_dim)/dynamic_update_slice | solution.py:70
  1249.2 46.1 %collective-permute-done = f32[192,2,512]{2,0,1:T(8,128)S(1)} collective-permute-done((f32[192,2,512]{2,0,1:T(8,128)S(1)}, f32[192,2,512]{2,0,1:T(8,128)S(1)}, u32[]{:S(2)}, u32[]{:S(2)}) %collective-permute-start) | collective-permute-done | bytes 786464 | tf_op jit(solution)/shard_map/ppermute | solution.py:12
  1304.6 17.8 %reduce-scatter.5.cloned.1.call-done = f32[48,9,192]{2,0,1:T(8,128)} async-done(((f32[384,9,192]{2,0,1:T(8,128)}), f32[48,9,192]{2,0,1:T(8,128)}) %reduce-scatter.5.cloned.1.call-update) | async-done | bytes 331792 | tf_op jit(solution)/shard_map/reduce_scatter | solution.py:33
  (301 shorter events, 790.7 us)
Async XLA Ops:
  7.2 1206.4 %copy-start = (bf16[9,192,2,512]{3,2,1,0:T(2,128)(2,1)S(1)}, bf16[9,192,2,512]{3,2,1,0:T(2,128)(2,1)}, u32[]{:S(2)}) copy-start(bf16[9,192,2,512]{3,2,1,0:T(2,128)(2,1)} %param.10) | copy-start | bytes 10616836
  7.2 1227.1 %reduce-scatter.3.cloned.1.call-start = ((), (), s32[]{:S(2)}) async-start(), calls=%async_computation.2 | async-start | bytes 11796480 | tf_op jit(solution)/shard_map/reduce_scatter | solution.py:80
  69.0 16.5 %copy-start.2 = (s32[2]{0:T(128)S(1)}, s32[2]{0:T(128)}, u32[]{:S(2)}) copy-start(s32[2]{0:T(128)} %param.15) | copy-start | bytes 28
  69.0 16.6 %copy-start.1 = (s32[2,16]{1,0:T(2,128)S(1)}, s32[2,16]{1,0:T(2,128)}, u32[]{:S(2)}) copy-start(s32[2,16]{1,0:T(2,128)} %param.14) | copy-start | bytes 388
  1213.5 108.9 %reduce-scatter.5.cloned.1.call-start = ((), (), s32[]{:S(2)}) async-start(), calls=%async_computation.3 | async-start | bytes 3981312 | tf_op jit(solution)/shard_map/reduce_scatter | solution.py:33
  1236.4 58.9 %collective-permute-start = (f32[192,2,512]{2,0,1:T(8,128)S(1)}, f32[192,2,512]{2,0,1:T(8,128)S(1)}, u32[]{:S(2)}, u32[]{:S(2)}) collective-permute-start(f32[192,2,512]{2,0,1:T(8,128)S(1)} %get-tuple-element.142), channel_id=1, source_target_pairs={{8,0},{12,4},{9,1},{13,5},{10,2},{14,6},{11,3},{15,7},{24,16},{28,... | collective-permute-start | bytes 2359304 | tf_op jit(solution)/shard_map/ppermute | solution.py:12
  1237.7 57.6 %collective-permute-start.1 = (f32[192,2,512]{2,0,1:T(8,128)S(1)}, f32[192,2,512]{2,0,1:T(8,128)S(1)}, u32[]{:S(2)}, u32[]{:S(2)}) collective-permute-start(f32[192,2,512]{2,0,1:T(8,128)S(1)} %get-tuple-element.145), channel_id=1, source_target_pairs={{4,0},{8,4},{12,8},{5,1},{9,5},{13,9},{6,2},{10,6},{14,10},{7,3},{... | collective-permute-start | bytes 2359304 | tf_op jit(solution)/shard_map/ppermute | solution.py:12
  1239.0 56.3 %collective-permute-start.2 = (f32[192,2,512]{2,0,1:T(8,128)S(1)}, f32[192,2,512]{2,0,1:T(8,128)S(1)}, u32[]{:S(2)}, u32[]{:S(2)}) collective-permute-start(f32[192,2,512]{2,0,1:T(8,128)S(1)} %get-tuple-element.144), channel_id=1, source_target_pairs={{0,4},{4,8},{8,12},{1,5},{5,9},{9,13},{2,6},{6,10},{10,14},{3,7},{... | collective-permute-start | bytes 2359304 | tf_op jit(solution)/shard_map/ppermute | solution.py:12
  1243.6 57.9 %collective-permute-start.3 = (f32[192,2,512]{2,0,1:T(8,128)S(1)}, f32[192,2,512]{2,0,1:T(8,128)S(1)}, u32[]{:S(2)}, u32[]{:S(2)}) collective-permute-start(f32[192,2,512]{2,0,1:T(8,128)S(1)} %get-tuple-element.143), channel_id=1, source_target_pairs={{0,8},{4,12},{1,9},{5,13},{2,10},{6,14},{3,11},{7,15},{16,24},{20,... | collective-permute-start | bytes 2359304 | tf_op jit(solution)/shard_map/ppermute | solution.py:12
Sparse Core Ops, SparseCore 0:
  1213.6 20.5 reduce-scatter.2
  1237.3 85.1 reduce-scatter.4
where the time goes:
time: 1360 us; the launch traced here: 1330 us
  local copies, waits for them, and re-layouts  939 us (69%)
  loops' own time  124 us (9%)
  other arithmetic  112 us (8%)
  waiting for transfers between devices  85.9 us (6%)
  matrix products  28.8 us (2%)
  between operations  14.1 us (1%)
    dynamic_update_slice x32, local copies, waits for them, and re-layouts, place_entry(): lax.dynamic_update_index_in_dim(summed, current + rolled, entry_targets[r...  508 us
    dynamic_slice x32, local copies, waits for them, and re-layouts, place_entry(): lax.dynamic_index_in_dim(summed, entry_targets[row], 1, keepdims=False)  130 us
    another operation x1, loops' own time, body(): lax.fori_loop(0, entries, place_entry, jnp.zeros((channels, window, cycle...  124 us
    dynamic_update_slice x32, local copies, waits for them, and re-layouts, place_entry(): lax.dynamic_update_slice(doubled, entry_pieces[row] * entry_live[row], (z...  113 us
    ppermute x4, waiting for transfers between devices, passed_along(): lax.ppermute(value, axis, [(source, source + steps) for source in range(i...  52.4 us
    mul x16, other arithmetic, place_entry(): entry_pieces[row] * entry_live[row]  52.1 us
    broadcast_in_dim x32, local copies, waits for them, and re-layouts, place_entry(): lax.dynamic_update_index_in_dim(summed, current + rolled, entry_targets[r...  49.7 us
    another operation x32, local copies, waits for them, and re-layouts  44.3 us
  transfers between devices with their start and end apart: 6, of which 4 were waited for; matrix products, arithmetic and copies ran while one was open for 1% of the time, Pallas kernels for 0%

commit v1 on v0

v1 whole, which is shorter than its diff:
```python
import functools

import jax
import jax.numpy as jnp
from jax import lax
from jax.experimental import pallas as pl
from jax.experimental.pallas import tpu as pltpu
from jax.sharding import PartitionSpec as P

HALO_DEV = 2
BLOCK = 64
LANES = 128


def quadrature_kernel(
    own_half, target, shift, lon, g_ref, w_ref, t_ref, far_ref, near_ref, acc, mixed, piece
):
    lon_halves, groups, rows, _, width = g_ref.shape
    window, cycle_blocks = acc.shape[0] - 1, acc.shape[1]
    entries = target.shape[1]
    basis = w_ref.shape[2] // LANES
    blocks = width // BLOCK
    pairs = cycle_blocks // 2
    acc[...] = jnp.zeros_like(acc)
    for row in range(rows):
        for half in range(lon_halves):
            total = None
            for group in range(groups):
                term = lax.dot_general(
                    g_ref[half, group, row],
                    w_ref[group],
                    (((0,), (0,)), ((), ())),
                    preferred_element_type=jnp.float32,
                )
                total = term if total is None else total + term
            total = total.astype(jnp.bfloat16)
            for block in range(blocks):
                at = half * blocks + block
                for k in range(basis):
                    mixed[
                        at // 2,
                        k * BLOCK : (k + 1) * BLOCK,
                        (at % 2) * LANES : (at % 2 + 1) * LANES,
                    ] = total[block * BLOCK : (block + 1) * BLOCK, k * LANES : (k + 1) * LANES]

        @pl.loop(0, pairs)
        def _(pair):
            piece[...] = jnp.dot(
                t_ref[row], mixed[pair], preferred_element_type=jnp.float32
            )
            for entry in range(entries):
                for side in range(2):
                    place = lax.rem(2 * pair + side + shift[row, entry], cycle_blocks)
                    acc[target[row, entry], place] += piece[
                        entry * BLOCK : (entry + 1) * BLOCK, side * LANES : (side + 1) * LANES
                    ]

    mid = window // rows // 2
    for at in range(window):
        step, row = at // rows, at % rows
        for side in range(2):
            half = lax.rem(lon[0] + side, 2)
            turned = acc[at, pl.ds(half * blocks, blocks)].reshape(width, LANES).T[:own_half]
            if step == mid:
                near_ref[side, row] = turned
            else:
                far_ref[step - (step > mid), side, row] = turned.astype(jnp.bfloat16)


def quadrature(own_half, target, shift, lon, g, w, t, window):
    lon_halves, groups, rows, _, width = g.shape
    cycle_blocks = lon_halves * width // BLOCK
    depth = t.shape[2]
    vmem = pl.BlockSpec(memory_space=pltpu.VMEM)
    smem = pl.BlockSpec(memory_space=pltpu.SMEM)
    return pl.pallas_call(
        functools.partial(quadrature_kernel, own_half),
        out_shape=(
            jax.ShapeDtypeStruct(
                (window // rows - 1, 2, rows, own_half, width), jnp.bfloat16
            ),
            jax.ShapeDtypeStruct((2, rows, own_half, width), jnp.float32),
        ),
        in_specs=[smem, smem, smem, vmem, vmem, vmem],
        out_specs=(vmem, vmem),
        scratch_shapes=[
            pltpu.VMEM((window + 1, cycle_blocks, BLOCK, LANES), jnp.float32),
            pltpu.VMEM((cycle_blocks // 2, depth, 2 * LANES), jnp.bfloat16),
            pltpu.VMEM((t.shape[1], 2 * LANES), jnp.float32),
        ],
        compiler_params=pltpu.CompilerParams(vmem_limit_bytes=48 * 1024 * 1024),
        cost_estimate=pl.CostEstimate(
            flops=9 * 10**9, bytes_accessed=10 * 2**20, transcendentals=0
        ),
    )(target, shift, lon, g, w, t)


def filter_gradient(full_out, saved_basis):
    product = jnp.einsum(
        "crow,kirw->coki", full_out, saved_basis, preferred_element_type=jnp.float32
    )
    groups, per, basis, channels = product.shape
    lat_devices = lax.axis_size("lat")
    lon_devices = lax.axis_size("lon")
    own_rows = groups * per // (lat_devices * lon_devices)
    if lat_devices > 8 or lon_devices != 2:
        return lax.psum_scatter(
            product.reshape(groups * per, basis, channels),
            ("lat", "lon"),
            scatter_dimension=0,
            tiled=True,
        )
    lat = lax.axis_index("lat")
    lon = lax.axis_index("lon")
    product = product.reshape(lat_devices, 2, own_rows, basis, channels)
    kept = lax.dynamic_index_in_dim(product, lon, 1, keepdims=False)
    given = lax.dynamic_index_in_dim(product, 1 - lon, 1, keepdims=False)
    kept = kept + lax.ppermute(given.astype(jnp.bfloat16), "lon", [(0, 1), (1, 0)])
    result = lax.dynamic_index_in_dim(kept, lat, 0, keepdims=False)
    narrow = kept.astype(jnp.bfloat16)
    for step in range(1, lat_devices):
        sent = lax.dynamic_index_in_dim(
            narrow, lax.rem(lat + step, lat_devices), 0, keepdims=False
        )
        result = result + lax.ppermute(
            sent, "lat", [(at, (at + step) % lat_devices) for at in range(lat_devices)]
        )
    return result


def body(grad_out, saved_basis, weight, quad_tiles, col_rows, col_shift, block_count):
    channels, rows, width = grad_out.shape
    basis = saved_basis.shape[0]
    out_channels = weight.shape[0]
    entries = quad_tiles.shape[1]
    lat_devices = lax.axis_size("lat")
    lat = lax.axis_index("lat")
    lon = lax.axis_index("lon")
    groups = out_channels // channels
    own_half = channels // 2
    window = (2 * HALO_DEV + 1) * rows

    full_out = lax.all_gather(grad_out.transpose(1, 0, 2), "ch", axis=0, tiled=False)
    grad_weight = filter_gradient(full_out, saved_basis)

    whole_out = lax.all_gather(full_out, "lon", axis=0, tiled=False)
    own_weight = lax.dynamic_slice_in_dim(weight, lon * own_half, own_half, 2)
    own_weight = jnp.pad(own_weight, ((0, 0), (0, 0), (0, LANES - own_half)))
    own_weight = own_weight.reshape(groups, channels, basis * LANES)
    turned = quad_tiles.transpose(0, 1, 4, 2, 3).reshape(rows, entries * BLOCK, basis * BLOCK)
    live = jnp.arange(entries, dtype=jnp.int32)[None, :] < block_count[:, None]
    target = jnp.where(live, col_rows - (lat - HALO_DEV) * rows, window)
    far, near = quadrature(
        own_half, target, col_shift, lon[None].astype(jnp.int32), whole_out, own_weight, turned, window
    )

    same = near[0]
    other = lax.ppermute(near[1], "lon", [(0, 1), (1, 0)])
    offsets = [step for step in range(-HALO_DEV, HALO_DEV + 1) if step != 0]
    for at, offset in enumerate(offsets):
        reach = [
            (source, source + offset)
            for source in range(lat_devices)
            if 0 <= source + offset < lat_devices
        ]
        same = same + lax.ppermute(far[at, 0], "lat", reach)
        other = other + lax.ppermute(
            far[at, 1],
            ("lat", "lon"),
            [(2 * a + c, 2 * b + 1 - c) for a, b in reach for c in range(2)],
        )
    first = jnp.where(lon == 0, same, other)
    second = jnp.where(lon == 0, other, same)
    grad_input = jnp.concatenate([first, second], axis=1).transpose(1, 0, 2)
    return (grad_input, grad_weight)


def solution(mesh):
    in_specs = (
        P("ch", ("grp", "lat"), "lon"),
        P(None, "ch", ("grp", "lat"), "lon"),
        P(None, None, "ch"),
        P("lat", None, None, None, None),
        P("lat", None),
        P("lat", None),
        P("lat"),
    )
    out_specs = (P("ch", ("grp", "lat"), "lon"), P(("grp", "lat", "lon"), None, "ch"))
    return jax.shard_map(body, mesh=mesh, in_specs=in_specs, out_specs=out_specs, check_vma=False)
```

time: 1360 us -> 134 us (0.10)
  the two profiles are of different devices: /device:TPU:0 before, /device:TPU:31 now
where the time goes in v1:
time: 134 us; the launch traced here: 133 us
  local copies, waits for them, and re-layouts  41.8 us (31%)
  starting transfers between devices  28.6 us (21%)
  Pallas kernels  15.4 us (11%)
  between operations  14.2 us (11%)
  waiting for transfers between devices  12.2 us (9%)
  blocking collectives  10.8 us (8%)
  other arithmetic  7.36 us (5%)
  matrix products  3.14 us (2%)
    pallas_call x1, Pallas kernels, quadrature(): pl.pallas_call(functools.partial(quadrature_kernel, own_half), out_shape=...  15.4 us
    ppermute x4, starting transfers between devices, body(): lax.ppermute(far[at, 1], ('lat', 'lon'), [(2 * a + c, 2 * b + 1 - c) for...  13 us
    ppermute x4, waiting for transfers between devices, body(): lax.ppermute(far[at, 1], ('lat', 'lon'), [(2 * a + c, 2 * b + 1 - c) for...  12.2 us
    reshape x2, local copies, waits for them, and re-layouts, body(): quad_tiles.transpose(0, 1, 4, 2, 3)  11.8 us
    ppermute x4, starting transfers between devices, body(): same = same + lax.ppermute(far[at, 0], 'lat', reach)  11.1 us
    all_gather x1, blocking collectives, body(): lax.all_gather(grad_out.transpose(1, 0, 2), 'ch', axis=0, tiled=False)  10.8 us
    transpose x1, local copies, waits for them, and re-layouts, body(): quad_tiles.transpose(0, 1, 4, 2, 3)  8.55 us
    reshape x2, local copies, waits for them, and re-layouts, body(): own_weight = own_weight.reshape(groups, channels, basis * LANES)  8.25 us
  transfers between devices with their start and end apart: 14, of which 2 were waited for; matrix products, arithmetic and copies ran while one was open for 33% of the time, Pallas kernels for 12%

profile of v1, /device:TPU:31, one launch (start us, length us, event | category | flops | bytes accessed | tf_op | source)
XLA Modules:
  0.0 133.5 jit_solution(18293615060289243477)
XLA Ops:
  8.4 10.8 %all-gather = bf16[4,192,512]{2,1,0:T(8,128)(2,1)} all-gather(bf16[2,192,512]{2,1,0:T(8,128)(2,1)S(1)} %bitcast.76), channel_id=2, replica_groups=mesh['grp'=2,'lat'=4,'ch'=2,'lon'=2] {'ch'}, dimensions={0}, use_global_device_ids=true | all-gather | bytes 1179648 | tf_op jit(solution)/shard_map/all_gather | solution.py:143
  19.2 3.1 %fusion = f32[2,192,9,192,1]{3,1,4,0,2:T(8,128)S(1)} fusion(bf16[2,2,192,512,1]{3,2,1,0,4:T(8,128)(2,1)} %bitcast.73, bf16[9,192,2,512,1]{3,2,1,0,4:T(2,128)(2,1)S(1)} %bitcast.69), kind=kOutput, calls=%fused_computation | convolution fusion | flops 1358954496 | bytes 6979584 | tf_op jit(solution)/shard_map/crow,kirw->coki/dot_general | solution.py:99
  22.4 1.8 %copy-done.5 = f32[2,192,9,192,1]{3,1,4,0,2:T(8,128)} copy-done((f32[2,192,9,192,1]{3,1,4,0,2:T(8,128)}, f32[2,192,9,192,1]{3,1,4,0,2:T(8,128)S(1)}, u32[]{:S(2)}) %copy-start.5) | copy-done | bytes 2654232
  25.2 1.6 %collective-permute-start.9 = (bf16[4,48,9,192]{3,1,0,2:T(8,128)(2,1)}, bf16[4,48,9,192]{3,1,0,2:T(8,128)(2,1)}, u32[]{:S(2)}, u32[]{:S(2)}) collective-permute-start(bf16[4,48,9,192]{3,1,0,2:T(8,128)(2,1)} %fusion.2), channel_id=1, source_target_pairs={{0,1},{1,0},{2,3},{3,2},{4,5},{5,4},{6,7},{7,6},{8,9},{9,8},{10,11... | collective-permute-start | bytes 1990664 | tf_op jit(solution)/shard_map/ppermute | solution.py:118
  29.0 4.1 %reshape.15 = bf16[2,192,1152]{1,0,2:T(2,128)(2,1)} reshape(bf16[384,9,128]{0,2,1:T(8,128)(2,1)} %pad.4) | data formatting | bytes 1769472 | tf_op jit(solution)/shard_map/reshape | solution.py:149
  33.2 4.1 %copy.23.w_ref = bf16[2,192,1152]{2,1,0:T(8,128)(2,1)} copy(bf16[2,192,1152]{1,0,2:T(2,128)(2,1)} %reshape.15) | data formatting | bytes 1769472 | tf_op jit(solution)/shard_map/reshape | solution.py:149
  37.3 8.5 %copy.22 = bf16[2,16,64,9,64]{2,1,4,3,0:T(8,128)(2,1)} copy(bf16[2,16,64,9,64]{2,4,3,1,0:T(8,128)(2,1)} %bitcast.71) | data formatting | bytes 4718592 | tf_op jit(solution)/shard_map/transpose | solution.py:150
  45.8 7.4 %reshape.16 = bf16[2,1024,576]{1,2,0:T(8,128)(2,1)} reshape(bf16[2,16,64,9,64]{2,1,4,3,0:T(8,128)(2,1)} %copy.22) | data formatting | bytes 4718592 | tf_op jit(solution)/shard_map/reshape | solution.py:150
  53.2 4.4 %copy.24.t_ref = bf16[2,1024,576]{2,1,0:T(8,128)(2,1)} copy(bf16[2,1024,576]{1,2,0:T(8,128)(2,1)} %reshape.16) | data formatting | bytes 4718592 | tf_op jit(solution)/shard_map/reshape | solution.py:150
  57.7 3.3 %fusion.8 = (bf16[4,48,9,192]{3,1,0,2:T(8,128)(2,1)S(1)}, f32[4,48,9,192]{3,1,0,2:T(8,128)}) fusion(bf16[4,48,9,192]{3,1,0,2:T(8,128)(2,1)} %collective-permute-done.9, f32[4,2,48,9,192]{4,2,1,0,3:T(8,128)} %bitcast.75, s32[]{:T(128)S(6)} %select_n.45), kind=kLoop, calls=%fused_computation.31 | loop fusion | flops 995328 | bytes 3981316 | tf_op jit(solution)/shard_map/convert_element_type | solution.py:120
  61.9 1.4 %collective-permute-start.11 = (bf16[48,9,192]{2,0,1:T(8,128)(2,1)}, bf16[48,9,192]{2,0,1:T(8,128)(2,1)}, u32[]{:S(2)}, u32[]{:S(2)}) collective-permute-start(bf16[48,9,192]{2,0,1:T(8,128)(2,1)} %get-tuple-element.26), channel_id=1, source_target_pairs={{0,8},{4,12},{8,0},{12,4},{1,9},{5,13},{9,1},{13,5},{2,10},{6,14},... | collective-permute-start | bytes 497672 | tf_op jit(solution)/shard_map/ppermute | solution.py:125
  64.6 1.4 %copy-done.3 = bf16[4,2,192,512]{3,2,1,0:T(8,128)(2,1)S(1)} copy-done((bf16[4,2,192,512]{3,2,1,0:T(8,128)(2,1)S(1)}, bf16[4,2,192,512]{3,2,1,0:T(8,128)(2,1)}, u32[]{:S(2)}) %copy-start.3) | copy-done | bytes 1572888
  66.0 15.4 %shard_map.86 = (bf16[4,2,2,96,512]{4,3,2,1,0:T(8,128)(2,1)S(1)}, f32[2,2,96,512]{3,2,1,0:T(8,128)S(1)}) custom-call(s32[2,16]{1,0:T(2,128)S(1)} %compare_select_fusion.target, s32[2,16]{1,0:T(2,128)S(1)} %copy-done.4, s32[1]{0:T(128)} %bitcast.lon, bf16[2,2,2,192,512]{4,3,2,1,0:T(8,128)(2,1)S(1)} %bitcast.70, bf16[2,192,1152]{2,1,0:T(8,128)(2,1)S(1)} %copy-done.1, ...), custom_call_target="tpu_custom_call" | custom-call | flops 8999999488 | bytes 10485760 | tf_op jit(solution)/shard_map/pallas_call | solution.py:76
  82.6 4.9 %collective-permute-start = (bf16[2,96,512]{2,1,0:T(8,128)(2,1)}, bf16[2,96,512]{2,1,0:T(8,128)(2,1)}, u32[]{:S(2)}, u32[]{:S(2)}) collective-permute-start(bf16[2,96,512]{2,1,0:T(8,128)(2,1)} %get-tuple-element.16), channel_id=1, source_target_pairs={{8,0},{12,4},{9,1},{13,5},{10,2},{14,6},{11,3},{15,7},{24,16},{28,... | collective-permute-start | bytes 589832 | tf_op jit(solution)/shard_map/ppermute | solution.py:166
  87.5 3.7 %collective-permute-start.1 = (bf16[2,96,512]{2,1,0:T(8,128)(2,1)}, bf16[2,96,512]{2,1,0:T(8,128)(2,1)}, u32[]{:S(2)}, u32[]{:S(2)}) collective-permute-start(bf16[2,96,512]{2,1,0:T(8,128)(2,1)} %get-tuple-element.23), channel_id=1, source_target_pairs={{4,0},{8,4},{12,8},{5,1},{9,5},{13,9},{6,2},{10,6},{14,10},{7,3},{... | collective-permute-start | bytes 589832 | tf_op jit(solution)/shard_map/ppermute | solution.py:166
  92.5 1.3 collective-permute-start.3
  94.6 1.4 %collective-permute-start.4 = (f32[2,96,512]{2,1,0:T(8,128)}, f32[2,96,512]{2,1,0:T(8,128)}, u32[]{:S(2)}, u32[]{:S(2)}) collective-permute-start(f32[2,96,512]{2,1,0:T(8,128)} %slice_bitcast_fusion), channel_id=1, source_target_pairs={{0,1},{1,0},{2,3},{3,2},{4,5},{5,4},{6,7},{7,6},{8,9},{9,8},{10,11... | collective-permute-start | bytes 1179656 | tf_op jit(solution)/shard_map/ppermute | solution.py:158
  96.0 5.7 %collective-permute-start.5 = (bf16[2,96,512]{2,1,0:T(8,128)(2,1)}, bf16[2,96,512]{2,1,0:T(8,128)(2,1)S(1)}, u32[]{:S(2)}, u32[]{:S(2)}) collective-permute-start(bf16[2,96,512]{2,1,0:T(8,128)(2,1)} %get-tuple-element.20), channel_id=1, source_target_pairs={{8,1},{9,0},{12,5},{13,4},{10,3},{11,2},{14,7},{15,6},{24,17},{25,... | collective-permute-start | bytes 589832 | tf_op jit(solution)/shard_map/ppermute | solution.py:167
  101.7 4.7 %collective-permute-start.6 = (bf16[2,96,512]{2,1,0:T(8,128)(2,1)}, bf16[2,96,512]{2,1,0:T(8,128)(2,1)S(1)}, u32[]{:S(2)}, u32[]{:S(2)}) collective-permute-start(bf16[2,96,512]{2,1,0:T(8,128)(2,1)} %get-tuple-element.19), channel_id=1, source_target_pairs={{4,1},{5,0},{8,5},{9,4},{12,9},{13,8},{6,3},{7,2},{10,7},{11,6},{1... | collective-permute-start | bytes 589832 | tf_op jit(solution)/shard_map/ppermute | solution.py:167
  109.0 2.2 %fusion.4 = f32[48,9,192]{2,0,1:T(8,128)} fusion(bf16[48,9,192]{2,0,1:T(8,128)(2,1)} %collective-permute-done.12, bf16[48,9,192]{2,0,1:T(8,128)(2,1)} %collective-permute-done.11, bf16[48,9,192]{2,0,1:T(8,128)(2,1)} %collective-permute-done.10, f32[4,48,9,192]{3,1,0,2:T(8,128)} %get-tuple-element.13, s32[]{:T(128)S(6)} %select_n.47), kind=kLoop, calls=%fused_computation.8 | loop fusion | flops 497664 | bytes 1161220 | tf_op jit(solution)/shard_map/add | solution.py:125
  111.2 4.6 %collective-permute-done.7 = bf16[2,96,512]{2,1,0:T(8,128)(2,1)S(1)} collective-permute-done((bf16[2,96,512]{2,1,0:T(8,128)(2,1)}, bf16[2,96,512]{2,1,0:T(8,128)(2,1)S(1)}, u32[]{:S(2)}, u32[]{:S(2)}) %collective-permute-start.7) | collective-permute-done | bytes 196640 | tf_op jit(solution)/shard_map/ppermute | solution.py:167
  115.8 7.6 %collective-permute-done.8 = bf16[2,96,512]{2,1,0:T(8,128)(2,1)S(1)} collective-permute-done((bf16[2,96,512]{2,1,0:T(8,128)(2,1)}, bf16[2,96,512]{2,1,0:T(8,128)(2,1)S(1)}, u32[]{:S(2)}, u32[]{:S(2)}) %collective-permute-start.8) | collective-permute-done | bytes 196640 | tf_op jit(solution)/shard_map/ppermute | solution.py:167
  123.4 1.7 %broadcast_select_fusion.1 = (f32[2,96,512]{2,1,0:T(8,128)S(1)}, f32[2,96,512]{2,1,0:T(8,128)S(1)}) fusion(pred[]{:T(512)S(6)} %eq.4, bf16[2,96,512]{2,1,0:T(8,128)(2,1)S(1)} %collective-permute-done.8, bf16[2,96,512]{2,1,0:T(8,128)(2,1)S(1)} %collective-permute-done.7, bf16[2,96,512]{2,1,0:T(8,128)(2,1)S(1)} %collective-permute-done.6, ...), kind=kLoop, calls=%fused_computation.28 | loop fusion | flops 1769472 | bytes 3145729 | tf_op jit(solution)/shard_map/jit(_where)/select_n | solution.py:172
  125.2 1.5 %copy.27 = f32[192,2,512]{2,1,0:T(2,128)} copy(f32[192,2,512]{2,0,1:T(8,128)S(1)} %maximum_bitcast_fusion) | data formatting | bytes 1572864
  (42 shorter events, 12.8 us)
Async XLA Ops:
  7.2 12.1 %copy-start = (bf16[9,192,2,512]{3,2,1,0:T(2,128)(2,1)S(1)}, bf16[9,192,2,512]{3,2,1,0:T(2,128)(2,1)}, u32[]{:S(2)}) copy-start(bf16[9,192,2,512]{3,2,1,0:T(2,128)(2,1)} %param.8) | copy-start | bytes 10616836
  7.2 56.2 %all-gather.4.cloned.1.call-start = ((), (), s32[]{:S(2)}) async-start(), calls=%async_computation | async-start | bytes 2359296 | tf_op jit(solution)/shard_map/all_gather | solution.py:146
  22.4 1.8 %copy-start.5 = (f32[2,192,9,192,1]{3,1,4,0,2:T(8,128)}, f32[2,192,9,192,1]{3,1,4,0,2:T(8,128)S(1)}, u32[]{:S(2)}) copy-start(f32[2,192,9,192,1]{3,1,4,0,2:T(8,128)S(1)} %fusion) | copy-start | bytes 7962628
  25.2 32.5 %collective-permute-start.9 = (bf16[4,48,9,192]{3,1,0,2:T(8,128)(2,1)}, bf16[4,48,9,192]{3,1,0,2:T(8,128)(2,1)}, u32[]{:S(2)}, u32[]{:S(2)}) collective-permute-start(bf16[4,48,9,192]{3,1,0,2:T(8,128)(2,1)} %fusion.2), channel_id=1, source_target_pairs={{0,1},{1,0},{2,3},{3,2},{4,5},{5,4},{6,7},{7,6},{8,9},{9,8},{10,11... | collective-permute-start | bytes 1990664 | tf_op jit(solution)/shard_map/ppermute | solution.py:118
  53.2 4.4 %copy-start.6 = (s32[2,16]{1,0:T(2,128)S(1)}, s32[2,16]{1,0:T(2,128)}, u32[]{:S(2)}) copy-start(s32[2,16]{1,0:T(2,128)} %param.11) | copy-start | bytes 388
  53.2 4.4 %copy-start.7 = (s32[2]{0:T(128)S(1)}, s32[2]{0:T(128)}, u32[]{:S(2)}) copy-start(s32[2]{0:T(128)} %param.13) | copy-start | bytes 28
  57.7 5.7 %copy-start.4 = (s32[2,16]{1,0:T(2,128)S(1)}, s32[2,16]{1,0:T(2,128)}, u32[]{:S(2)}) copy-start(s32[2,16]{1,0:T(2,128)} %shift.1) | copy-start | bytes 388
  61.9 29.3 %collective-permute-start.10 = (bf16[48,9,192]{2,0,1:T(8,128)(2,1)}, bf16[48,9,192]{2,0,1:T(8,128)(2,1)}, u32[]{:S(2)}, u32[]{:S(2)}) collective-permute-start(bf16[48,9,192]{2,0,1:T(8,128)(2,1)} %get-tuple-element.24), channel_id=1, source_target_pairs={{0,4},{4,8},{8,12},{12,0},{1,5},{5,9},{9,13},{13,1},{2,6},{6,10},{... | collective-permute-start | bytes 497672 | tf_op jit(solution)/shard_map/ppermute | solution.py:125
  61.9 30.6 %collective-permute-start.11 = (bf16[48,9,192]{2,0,1:T(8,128)(2,1)}, bf16[48,9,192]{2,0,1:T(8,128)(2,1)}, u32[]{:S(2)}, u32[]{:S(2)}) collective-permute-start(bf16[48,9,192]{2,0,1:T(8,128)(2,1)} %get-tuple-element.26), channel_id=1, source_target_pairs={{0,8},{4,12},{8,0},{12,4},{1,9},{5,13},{9,1},{13,5},{2,10},{6,14},... | collective-permute-start | bytes 497672 | tf_op jit(solution)/shard_map/ppermute | solution.py:125
  63.2 31.4 %collective-permute-start.12 = (bf16[48,9,192]{2,0,1:T(8,128)(2,1)}, bf16[48,9,192]{2,0,1:T(8,128)(2,1)}, u32[]{:S(2)}, u32[]{:S(2)}) collective-permute-start(bf16[48,9,192]{2,0,1:T(8,128)(2,1)} %get-tuple-element.25), channel_id=1, source_target_pairs={{0,12},{4,0},{8,4},{12,8},{1,13},{5,1},{9,5},{13,9},{2,14},{6,2},{... | collective-permute-start | bytes 497672 | tf_op jit(solution)/shard_map/ppermute | solution.py:125
  63.4 1.2 copy-start.1
  64.6 1.4 %copy-start.3 = (bf16[4,2,192,512]{3,2,1,0:T(8,128)(2,1)S(1)}, bf16[4,2,192,512]{3,2,1,0:T(8,128)(2,1)}, u32[]{:S(2)}) copy-start(bf16[4,2,192,512]{3,2,1,0:T(8,128)(2,1)} %all-gather.4.cloned.1.call-done) | copy-start | bytes 4718596
  81.4 12.4 %copy-start.2 = (f32[2,2,96,512]{3,2,1,0:T(8,128)}, f32[2,2,96,512]{3,2,1,0:T(8,128)S(1)}, u32[]{:S(2)}) copy-start(f32[2,2,96,512]{3,2,1,0:T(8,128)S(1)} %get-tuple-element.4) | copy-start | bytes 2359300
  82.6 13.4 %collective-permute-start = (bf16[2,96,512]{2,1,0:T(8,128)(2,1)}, bf16[2,96,512]{2,1,0:T(8,128)(2,1)}, u32[]{:S(2)}, u32[]{:S(2)}) collective-permute-start(bf16[2,96,512]{2,1,0:T(8,128)(2,1)} %get-tuple-element.16), channel_id=1, source_target_pairs={{8,0},{12,4},{9,1},{13,5},{10,2},{14,6},{11,3},{15,7},{24,16},{28,... | collective-permute-start | bytes 589832 | tf_op jit(solution)/shard_map/ppermute | solution.py:166
  87.5 14.2 %collective-permute-start.1 = (bf16[2,96,512]{2,1,0:T(8,128)(2,1)}, bf16[2,96,512]{2,1,0:T(8,128)(2,1)}, u32[]{:S(2)}, u32[]{:S(2)}) collective-permute-start(bf16[2,96,512]{2,1,0:T(8,128)(2,1)} %get-tuple-element.23), channel_id=1, source_target_pairs={{4,0},{8,4},{12,8},{5,1},{9,5},{13,9},{6,2},{10,6},{14,10},{7,3},{... | collective-permute-start | bytes 589832 | tf_op jit(solution)/shard_map/ppermute | solution.py:166
  91.2 15.2 %collective-permute-start.2 = (bf16[2,96,512]{2,1,0:T(8,128)(2,1)}, bf16[2,96,512]{2,1,0:T(8,128)(2,1)}, u32[]{:S(2)}, u32[]{:S(2)}) collective-permute-start(bf16[2,96,512]{2,1,0:T(8,128)(2,1)} %get-tuple-element.22), channel_id=1, source_target_pairs={{0,4},{4,8},{8,12},{1,5},{5,9},{9,13},{2,6},{6,10},{10,14},{3,7},{... | collective-permute-start | bytes 589832 | tf_op jit(solution)/shard_map/ppermute | solution.py:166
  92.5 15.2 %collective-permute-start.3 = (bf16[2,96,512]{2,1,0:T(8,128)(2,1)}, bf16[2,96,512]{2,1,0:T(8,128)(2,1)}, u32[]{:S(2)}, u32[]{:S(2)}) collective-permute-start(bf16[2,96,512]{2,1,0:T(8,128)(2,1)} %get-tuple-element.21), channel_id=1, source_target_pairs={{0,8},{4,12},{1,9},{5,13},{2,10},{6,14},{3,11},{7,15},{16,24},{20,... | collective-permute-start | bytes 589832 | tf_op jit(solution)/shard_map/ppermute | solution.py:166
  94.6 28.8 %collective-permute-start.4 = (f32[2,96,512]{2,1,0:T(8,128)}, f32[2,96,512]{2,1,0:T(8,128)}, u32[]{:S(2)}, u32[]{:S(2)}) collective-permute-start(f32[2,96,512]{2,1,0:T(8,128)} %slice_bitcast_fusion), channel_id=1, source_target_pairs={{0,1},{1,0},{2,3},{3,2},{4,5},{5,4},{6,7},{7,6},{8,9},{9,8},{10,11... | collective-permute-start | bytes 1179656 | tf_op jit(solution)/shard_map/ppermute | solution.py:158
  96.0 15.2 %collective-permute-start.5 = (bf16[2,96,512]{2,1,0:T(8,128)(2,1)}, bf16[2,96,512]{2,1,0:T(8,128)(2,1)S(1)}, u32[]{:S(2)}, u32[]{:S(2)}) collective-permute-start(bf16[2,96,512]{2,1,0:T(8,128)(2,1)} %get-tuple-element.20), channel_id=1, source_target_pairs={{8,1},{9,0},{12,5},{13,4},{10,3},{11,2},{14,7},{15,6},{24,17},{25,... | collective-permute-start | bytes 589832 | tf_op jit(solution)/shard_map/ppermute | solution.py:167
  101.7 9.5 %collective-permute-start.6 = (bf16[2,96,512]{2,1,0:T(8,128)(2,1)}, bf16[2,96,512]{2,1,0:T(8,128)(2,1)S(1)}, u32[]{:S(2)}, u32[]{:S(2)}) collective-permute-start(bf16[2,96,512]{2,1,0:T(8,128)(2,1)} %get-tuple-element.19), channel_id=1, source_target_pairs={{4,1},{5,0},{8,5},{9,4},{12,9},{13,8},{6,3},{7,2},{10,7},{11,6},{1... | collective-permute-start | bytes 589832 | tf_op jit(solution)/shard_map/ppermute | solution.py:167
  106.4 9.4 %collective-permute-start.7 = (bf16[2,96,512]{2,1,0:T(8,128)(2,1)}, bf16[2,96,512]{2,1,0:T(8,128)(2,1)S(1)}, u32[]{:S(2)}, u32[]{:S(2)}) collective-permute-start(bf16[2,96,512]{2,1,0:T(8,128)(2,1)} %get-tuple-element.18), channel_id=1, source_target_pairs={{0,5},{1,4},{4,9},{5,8},{8,13},{9,12},{2,7},{3,6},{6,11},{7,10},{1... | collective-permute-start | bytes 589832 | tf_op jit(solution)/shard_map/ppermute | solution.py:167
  107.7 15.7 %collective-permute-start.8 = (bf16[2,96,512]{2,1,0:T(8,128)(2,1)}, bf16[2,96,512]{2,1,0:T(8,128)(2,1)S(1)}, u32[]{:S(2)}, u32[]{:S(2)}) collective-permute-start(bf16[2,96,512]{2,1,0:T(8,128)(2,1)} %get-tuple-element.17), channel_id=1, source_target_pairs={{0,9},{1,8},{4,13},{5,12},{2,11},{3,10},{6,15},{7,14},{16,25},{17,... | collective-permute-start | bytes 589832 | tf_op jit(solution)/shard_map/ppermute | solution.py:167
Sparse Core Ops, SparseCore 0:
  19.3 12.3 all-gather.3

commit v2 on v1

--- a/solution.py
+++ b/solution.py
@@ -10,6 +10,219 @@
 HALO_DEV = 2
 BLOCK = 64
 LANES = 128
+
+
+MESH = pl.DeviceIdType.MESH
+ROOM = 48 * 1024 * 1024
+
+
+def gather_kernel(own_half, g_ref, q_hbm, k_hbm, whole, t_ref, w_ref, q_ref, k_ref, fetch, out_sem, in_sem):
+    groups = lax.axis_size("ch")
+    ch, lon = lax.axis_index("ch"), lax.axis_index("lon")
+    rows, entries, basis = q_ref.shape[0], q_ref.shape[1], q_ref.shape[2]
+    channels = g_ref.shape[1]
+    tiles = pltpu.make_async_copy(q_hbm, q_ref, fetch.at[0])
+    filters = pltpu.make_async_copy(k_hbm, k_ref, fetch.at[1])
+    tiles.start()
+    filters.start()
+    barrier = pltpu.get_barrier_semaphore()
+    for step in range(1, groups):
+        pl.semaphore_signal(
+            barrier, inc=1, device_id={"ch": lax.rem(ch + step, groups)}, device_id_type=MESH
+        )
+    pl.semaphore_signal(barrier, inc=1, device_id={"lon": 1 - lon}, device_id_type=MESH)
+    pl.semaphore_wait(barrier, groups)
+
+    across = [
+        pltpu.make_async_remote_copy(
+            src_ref=g_ref,
+            dst_ref=whole.at[0, ch],
+            send_sem=out_sem.at[step],
+            recv_sem=in_sem.at[step],
+            device_id={"ch": lax.rem(ch + step, groups)},
+            device_id_type=MESH,
+        )
+        for step in range(1, groups)
+    ]
+    for copy in across:
+        copy.start()
+
+    def beside(step):
+        source = lax.rem(ch + groups - step, groups)
+        return pltpu.make_async_remote_copy(
+            src_ref=g_ref if step == 0 else whole.at[0, source],
+            dst_ref=whole.at[1, source],
+            send_sem=out_sem.at[groups + step],
+            recv_sem=in_sem.at[groups + step],
+            device_id={"lon": 1 - lon},
+            device_id_type=MESH,
+        )
+
+    forward = [beside(step) for step in range(groups)]
+    forward[0].start()
+    whole[0, ch] = g_ref[...]
+
+    tiles.wait()
+    for row in range(rows):
+
+        @pl.loop(0, entries // 2)
+        def _(pair):
+            two = jnp.concatenate(
+                [
+                    q_ref[row, 2 * pair].reshape(basis * BLOCK, BLOCK),
+                    q_ref[row, 2 * pair + 1].reshape(basis * BLOCK, BLOCK),
+                ],
+                axis=1,
+            )
+            t_ref[row, pl.ds(pl.multiple_of(pair * 2 * BLOCK, 2 * BLOCK), 2 * BLOCK)] = two.T
+
+    filters.wait()
+    w_ref[...] = jnp.zeros_like(w_ref)
+    for half in range(2):
+
+        @pl.when(lon == half)
+        def _():
+            for k in range(basis):
+                for group in range(groups):
+                    w_ref[group, :, k * LANES : k * LANES + own_half] = k_ref[
+                        k,
+                        group * channels : (group + 1) * channels,
+                        half * own_half : (half + 1) * own_half,
+                    ]
+
+    for step in range(1, groups):
+        across[step - 1].wait_recv()
+        forward[step].start()
+    for copy in across:
+        copy.wait_send()
+    for copy in forward:
+        copy.wait()
+
+
+def gathered(own_half, turned_out, quad_tiles, weight):
+    rows, channels, width = turned_out.shape
+    entries, basis = quad_tiles.shape[1:3]
+    groups = lax.axis_size("ch")
+    vmem = pl.BlockSpec(memory_space=pltpu.VMEM)
+    far = pl.BlockSpec(memory_space=pl.ANY)
+    return pl.pallas_call(
+        functools.partial(gather_kernel, own_half),
+        out_shape=(
+            jax.ShapeDtypeStruct((2, groups, rows, channels, width), jnp.bfloat16),
+            jax.ShapeDtypeStruct((rows, entries * BLOCK, basis * BLOCK), jnp.bfloat16),
+            jax.ShapeDtypeStruct((groups, channels, basis * LANES), jnp.bfloat16),
+        ),
+        in_specs=[vmem, far, far],
+        out_specs=(vmem, vmem, vmem),
+        scratch_shapes=[
+            pltpu.VMEM(quad_tiles.shape, jnp.bfloat16),
+            pltpu.VMEM(weight.shape, jnp.bfloat16),
+            pltpu.SemaphoreType.DMA((2,)),
+            pltpu.SemaphoreType.DMA((2 * groups,)),
+            pltpu.SemaphoreType.DMA((2 * groups,)),
+        ],
+        compiler_params=pltpu.CompilerParams(
+            collective_id=0, has_side_effects=True, vmem_limit_bytes=ROOM
+        ),
+        cost_estimate=pl.CostEstimate(flops=0, bytes_accessed=10 * 2**20, transcendentals=0),
+    )(turned_out, quad_tiles, weight)
+
+
+def sum_kernel(far_ref, near_ref, out_ref, arrived, beside, out_sem, in_sem, pair_sem):
+    lat_devices = lax.axis_size("lat")
+    lat, lon = lax.axis_index("lat"), lax.axis_index("lon")
+    own_half = near_ref.shape[2]
+    offsets = [step for step in range(-HALO_DEV, HALO_DEV + 1) if step != 0]
+    order = sorted(range(len(offsets)), key=lambda at: abs(offsets[at]))
+
+    def reaches(step):
+        return jnp.logical_and(lat + step >= 0, lat + step < lat_devices)
+
+    barrier = pltpu.get_barrier_semaphore()
+    pl.semaphore_signal(barrier, inc=1, device_id={"lon": 1 - lon}, device_id_type=MESH)
+    for step in offsets:
+
+        @pl.when(reaches(step))
+        def _():
+            for side in range(2):
+                pl.semaphore_signal(
+                    barrier,
+                    inc=1,
+                    device_id={"lat": lat + step, "lon": lax.rem(lon + side, 2)},
+                    device_id_type=MESH,
+                )
+
+    pl.semaphore_wait(barrier, 1 + sum(jnp.where(reaches(step), 2, 0) for step in offsets))
+
+    def message(at, side):
+        return pltpu.make_async_remote_copy(
+            src_ref=far_ref.at[at, side],
+            dst_ref=arrived.at[at, side],
+            send_sem=out_sem.at[at, side],
+            recv_sem=in_sem.at[at, side],
+            device_id={"lat": lat + offsets[at], "lon": lax.rem(lon + side, 2)},
+            device_id_type=MESH,
+        )
+
+    pair = pltpu.make_async_remote_copy(
+        src_ref=near_ref.at[1],
+        dst_ref=beside,
+        send_sem=pair_sem.at[0],
+        recv_sem=pair_sem.at[1],
+        device_id={"lon": 1 - lon},
+        device_id_type=MESH,
+    )
+    for at in order:
+
+        @pl.when(reaches(offsets[at]))
+        def _():
+            for side in range(2):
+                message(at, side).start()
+
+    pair.start()
+    spans = [
+        pl.ds(pl.multiple_of(lax.rem(lon + side, 2) * own_half, 8), own_half) for side in range(2)
+    ]
+    out_ref[:, spans[0]] = near_ref[0]
+    pair.wait_recv()
+    out_ref[:, spans[1]] = beside[...]
+    for at in order:
+
+        @pl.when(reaches(-offsets[at]))
+        def _():
+            for side in range(2):
+                message(at, side).wait_recv()
+                out_ref[:, spans[side]] += arrived[at, side].astype(jnp.float32)
+
+    pair.wait_send()
+    for at in order:
+
+        @pl.when(reaches(offsets[at]))
+        def _():
+            for side in range(2):
+                message(at, side).wait_send()
+
+
+def summed(far, near):
+    _, rows, own_half, width = near.shape
+    vmem = pl.BlockSpec(memory_space=pltpu.VMEM)
+    return pl.pallas_call(
+        sum_kernel,
+        out_shape=jax.ShapeDtypeStruct((rows, 2 * own_half, width), jnp.float32),
+        in_specs=[vmem, vmem],
+        out_specs=vmem,
+        scratch_shapes=[
+            pltpu.VMEM(far.shape, jnp.bfloat16),
+            pltpu.VMEM(near.shape[1:], jnp.float32),
+            pltpu.SemaphoreType.DMA(far.shape[:2]),
+            pltpu.SemaphoreType.DMA(far.shape[:2]),
+            pltpu.SemaphoreType.DMA((2,)),
+        ],
+        compiler_params=pltpu.CompilerParams(
+            collective_id=1, has_side_effects=True, vmem_limit_bytes=ROOM
+        ),
+        cost_estimate=pl.CostEstimate(flops=0, bytes_accessed=40 * 2**20, transcendentals=0),
+    )(far, near)
 
 
 def quadrature_kernel(
@@ -34,13 +247,13 @@
                 )
                 total = term if total is None else total + term
             total = total.astype(jnp.bfloat16)
+            first = lax.rem(lon[0] + half, 2) * (blocks // 2)
             for block in range(blocks):
-                at = half * blocks + block
                 for k in range(basis):
                     mixed[
-                        at // 2,
+                        first + block // 2,
                         k * BLOCK : (k + 1) * BLOCK,
-                        (at % 2) * LANES : (at % 2 + 1) * LANES,
+                        (block % 2) * LANES : (block % 2 + 1) * LANES,
                     ] = total[block * BLOCK : (block + 1) * BLOCK, k * LANES : (k + 1) * LANES]
 
         @pl.loop(0, pairs)
@@ -88,7 +301,7 @@
             pltpu.VMEM((cycle_blocks // 2, depth, 2 * LANES), jnp.bfloat16),
             pltpu.VMEM((t.shape[1], 2 * LANES), jnp.float32),
         ],
-        compiler_params=pltpu.CompilerParams(vmem_limit_bytes=48 * 1024 * 1024),
+        compiler_params=pltpu.CompilerParams(vmem_limit_bytes=ROOM),
         cost_estimate=pl.CostEstimate(
             flops=9 * 10**9, bytes_accessed=10 * 2**20, transcendentals=0
         ),
@@ -130,48 +343,23 @@
 
 def body(grad_out, saved_basis, weight, quad_tiles, col_rows, col_shift, block_count):
     channels, rows, width = grad_out.shape
-    basis = saved_basis.shape[0]
-    out_channels = weight.shape[0]
     entries = quad_tiles.shape[1]
-    lat_devices = lax.axis_size("lat")
     lat = lax.axis_index("lat")
     lon = lax.axis_index("lon")
-    groups = out_channels // channels
     own_half = channels // 2
     window = (2 * HALO_DEV + 1) * rows
 
-    full_out = lax.all_gather(grad_out.transpose(1, 0, 2), "ch", axis=0, tiled=False)
-    grad_weight = filter_gradient(full_out, saved_basis)
-
-    whole_out = lax.all_gather(full_out, "lon", axis=0, tiled=False)
-    own_weight = lax.dynamic_slice_in_dim(weight, lon * own_half, own_half, 2)
-    own_weight = jnp.pad(own_weight, ((0, 0), (0, 0), (0, LANES - own_half)))
-    own_weight = own_weight.reshape(groups, channels, basis * LANES)
-    turned = quad_tiles.transpose(0, 1, 4, 2, 3).reshape(rows, entries * BLOCK, basis * BLOCK)
+    whole_out, turned, own_weight = gathered(
+        own_half, grad_out.transpose(1, 0, 2), quad_tiles, weight.transpose(1, 0, 2)
+    )
+    grad_weight = filter_gradient(whole_out[0], saved_basis)
     live = jnp.arange(entries, dtype=jnp.int32)[None, :] < block_count[:, None]
     target = jnp.where(live, col_rows - (lat - HALO_DEV) * rows, window)
     far, near = quadrature(
         own_half, target, col_shift, lon[None].astype(jnp.int32), whole_out, own_weight, turned, window
     )
 
-    same = near[0]
-    other = lax.ppermute(near[1], "lon", [(0, 1), (1, 0)])
-    offsets = [step for step in range(-HALO_DEV, HALO_DEV + 1) if step != 0]
-    for at, offset in enumerate(offsets):
-        reach = [
-            (source, source + offset)
-            for source in range(lat_devices)
-            if 0 <= source + offset < lat_devices
-        ]
-        same = same + lax.ppermute(far[at, 0], "lat", reach)
-        other = other + lax.ppermute(
-            far[at, 1],
-            ("lat", "lon"),
-            [(2 * a + c, 2 * b + 1 - c) for a, b in reach for c in range(2)],
-        )
-    first = jnp.where(lon == 0, same, other)
-    second = jnp.where(lon == 0, other, same)
-    grad_input = jnp.concatenate([first, second], axis=1).transpose(1, 0, 2)
+    grad_input = summed(far, near).transpose(1, 0, 2)
     return (grad_input, grad_weight)
 
 

time: 134 us -> 101 us (0.75)
  the two profiles are of different devices: /device:TPU:31 before, /device:TPU:0 now
where the time goes in v2:
time: 101 us
  Pallas kernels  61.4 us (61%)
  local copies, waits for them, and re-layouts  20.6 us (20%)
  other arithmetic  5.55 us (5%)
  starting transfers between devices  5 us (5%)
  matrix products  4.94 us (5%)
  waiting for transfers between devices  2.32 us (2%)
    pallas_call x1, Pallas kernels, summed(): pl.pallas_call(sum_kernel, out_shape=jax.ShapeDtypeStruct((rows, 2 * own_...  30 us
    unnamed x31, local copies, waits for them, and re-layouts  16.3 us
    pallas_call x1, Pallas kernels, gathered(): pl.pallas_call(functools.partial(gather_kernel, own_half), out_shape=(jax...  16 us
    pallas_call x1, Pallas kernels, quadrature(): pl.pallas_call(functools.partial(quadrature_kernel, own_half), out_shape=...  15.4 us
    dot_general x1, matrix products, filter_gradient(): jnp.einsum('crow,kirw->coki', full_out, saved_basis, preferred_element_ty...  4.94 us
    ppermute x3, starting transfers between devices, filter_gradient(): lax.ppermute(sent, 'lat', [(at, (at + step) % lat_devices) for at in rang...  4.63 us
    convert_element_type x1, other arithmetic, filter_gradient(): narrow = kept.astype(jnp.bfloat16)  3.28 us
    convert_element_type x1, local copies, waits for them, and re-layouts, filter_gradient(): given.astype(jnp.bfloat16)  2.52 us
  transfers between devices with their start and end apart: 4, of which 1 were waited for; matrix products, arithmetic and copies ran while one was open for 2% of the time, Pallas kernels for 45%

profile of v2, /device:TPU:0, one launch (start us, length us, event | category | flops | bytes accessed | tf_op | source)
XLA Modules:
  0.0 100.5 jit_solution(13874721564786813892)
XLA Ops:
  0.6 1.9 %copy.33 = bf16[192,2,512]{2,0,1:T(8,128)(2,1)} copy(bf16[192,2,512]{2,1,0:T(2,128)(2,1)} %param.7) | data formatting | bytes 786432 | tf_op args[0]
  2.6 3.6 %copy.14 = bf16[384,9,192]{2,0,1:T(8,128)(2,1)} copy(bf16[384,9,192]{0,2,1:T(8,128)(2,1)} %param.9) | data formatting | bytes 2654208 | tf_op args[2]
  6.2 1.5 %copy-done.1 = bf16[384,9,192]{2,0,1:T(8,128)(2,1)S(1)} copy-done((bf16[384,9,192]{2,0,1:T(8,128)(2,1)S(1)}, bf16[384,9,192]{2,0,1:T(8,128)(2,1)}, u32[]{:S(2)}) %copy-start.1) | copy-done | bytes 1327128
  7.7 1.0 copy-done.4
  8.7 16.0 %shard_map.86 = (bf16[2,2,2,192,512]{4,3,2,1,0:T(8,128)(2,1)S(1)}, bf16[2,1024,576]{2,1,0:T(8,128)(2,1)}, bf16[2,192,1152]{2,1,0:T(8,128)(2,1)S(1)}) custom-call(bf16[2,192,512]{2,1,0:T(8,128)(2,1)S(1)} %bitcast.37, bf16[2,16,9,64,64]{4,3,2,1,0:T(8,128)(2,1)} %q_hbm.1, bf16[9,384,192]{2,1,0:T(8,128)(2,1)S(1)} %bitcast.35), custom_call_target="tpu_custom_call" | custom-call | bytes 10485760 | tf_op jit(solution)/shard_map/pallas_call | solution.py:108
  24.8 0.8 copy-done.9
  25.7 1.3 %copy-done.7 = bf16[2,2,2,192,512]{4,3,2,1,0:T(8,128)(2,1)} copy-done((bf16[2,2,2,192,512]{4,3,2,1,0:T(8,128)(2,1)}, bf16[2,2,2,192,512]{4,3,2,1,0:T(8,128)(2,1)S(1)}, u32[]{:S(2)}) %copy-start.7) | copy-done | bytes 1572888
  26.9 0.9 copy.15
  27.9 4.9 %fusion.2 = f32[4,2,48,9,192]{4,2,3,1,0:T(8,128)} fusion(bf16[9,192,2,512,1,1]{3,2,1,0,5,4:T(2,128)(2,1)S(1)} %bitcast.34, bf16[4,2,48,2,512,1]{4,2,1,0,3,5:T(8,128)(2,1)} %bitcast.38), kind=kOutput, calls=%fused_computation.2 | convolution fusion | flops 1358954496 | bytes 6979584 | tf_op jit(solution)/shard_map/crow,kirw->coki/dot_general | solution.py:312
  32.8 2.5 %fusion.5 = bf16[4,48,9,192]{3,1,2,0:T(8,128)(2,1)} fusion(f32[4,2,48,9,192]{4,2,3,1,0:T(8,128)} %fusion.2, s32[]{:T(128)S(6)} %select_n.27), kind=kLoop, calls=%fused_computation.5 | loop fusion | bytes 1327108 | tf_op jit(solution)/shard_map/convert_element_type | solution.py:331
  35.3 0.4 collective-permute-start
  35.8 2.3 %collective-permute-done = bf16[4,48,9,192]{3,1,2,0:T(8,128)(2,1)} collective-permute-done((bf16[4,48,9,192]{3,1,2,0:T(8,128)(2,1)}, bf16[4,48,9,192]{3,1,2,0:T(8,128)(2,1)}, u32[]{:S(2)}, u32[]{:S(2)}) %collective-permute-start) | collective-permute-done | bytes 663584 | tf_op jit(solution)/shard_map/ppermute | solution.py:331
  38.1 3.3 %fusion.9 = (bf16[4,48,9,192]{3,1,2,0:T(8,128)(2,1)S(1)}, f32[4,48,9,192]{3,1,2,0:T(8,128)}) fusion(bf16[4,48,9,192]{3,1,2,0:T(8,128)(2,1)} %collective-permute-done, f32[4,2,48,9,192]{4,2,3,1,0:T(8,128)} %fusion.2, s32[]{:T(128)S(6)} %select_n.26), kind=kLoop, calls=%fused_computation.16 | loop fusion | flops 995328 | bytes 3981316 | tf_op jit(solution)/shard_map/convert_element_type | solution.py:333
  41.4 0.9 dynamic-slice_bitcast_fusion.2
  42.2 3.6 %collective-permute-start.3 = (bf16[48,9,192]{2,0,1:T(8,128)(2,1)}, bf16[48,9,192]{2,0,1:T(8,128)(2,1)}, u32[]{:S(2)}, u32[]{:S(2)}) collective-permute-start(bf16[48,9,192]{2,0,1:T(8,128)(2,1)} %get-tuple-element.19), channel_id=1, source_target_pairs={{0,12},{4,0},{8,4},{12,8},{1,13},{5,1},{9,5},{13,9},{2,14},{6,2},{... | collective-permute-start | bytes 497672 | tf_op jit(solution)/shard_map/ppermute | solution.py:338
  45.8 1.0 collective-permute-start.1
  46.9 15.4 %shard_map.87 = (bf16[4,2,2,96,512]{4,3,2,1,0:T(8,128)(2,1)S(1)}, f32[2,2,96,512]{3,2,1,0:T(8,128)S(1)}) custom-call(s32[2,16]{1,0:T(2,128)S(1)} %compare_select_fusion.target, s32[2,16]{1,0:T(2,128)S(1)} %copy-done.11, s32[1]{0:T(128)} %bitcast.lon, bf16[2,2,2,192,512]{4,3,2,1,0:T(8,128)(2,1)S(1)} %copy-done.8, bf16[2,192,1152]{2,1,0:T(8,128)(2,1)S(1)} %copy-done.10, ...), custom_call_target="tpu_custom_call" | custom-call | flops 8999999488 | bytes 10485760 | tf_op jit(solution)/shard_map/pallas_call | solution.py:289
  62.3 1.2 %copy-done.2 = bf16[4,2,2,96,512]{4,3,2,1,0:T(8,128)(2,1)} copy-done((bf16[4,2,2,96,512]{4,3,2,1,0:T(8,128)(2,1)}, bf16[4,2,2,96,512]{4,3,2,1,0:T(8,128)(2,1)S(1)}, u32[]{:S(2)}) %copy-start.2) | copy-done | bytes 1572888
  63.4 0.9 copy-done.5
  64.3 1.4 %copy-done.3 = bf16[4,2,2,96,512]{4,3,2,1,0:T(8,128)(2,1)S(1)} copy-done((bf16[4,2,2,96,512]{4,3,2,1,0:T(8,128)(2,1)S(1)}, bf16[4,2,2,96,512]{4,3,2,1,0:T(8,128)(2,1)}, u32[]{:S(2)}) %copy-start.3) | copy-done | bytes 1572888
  65.7 1.1 %copy-done.6 = f32[2,2,96,512]{3,2,1,0:T(8,128)S(1)} copy-done((f32[2,2,96,512]{3,2,1,0:T(8,128)S(1)}, f32[2,2,96,512]{3,2,1,0:T(8,128)}, u32[]{:S(2)}) %copy-start.6) | copy-done | bytes 786456
  66.9 30.0 %shard_map.88 = f32[2,192,512]{2,1,0:T(8,128)S(1)} custom-call(bf16[4,2,2,96,512]{4,3,2,1,0:T(8,128)(2,1)S(1)} %copy-done.3, f32[2,2,96,512]{3,2,1,0:T(8,128)S(1)} %copy-done.6), custom_call_target="tpu_custom_call" | custom-call | bytes 41943040 | tf_op jit(solution)/shard_map/pallas_call | solution.py:209
  96.8 1.5 %copy.18 = f32[192,2,512]{2,1,0:T(2,128)} copy(f32[192,2,512]{2,0,1:T(8,128)S(1)} %bitcast.36) | data formatting | bytes 1572864
  98.3 2.2 %fusion.8 = f32[48,9,192]{2,0,1:T(8,128)} fusion(bf16[48,9,192]{2,0,1:T(8,128)(2,1)} %collective-permute-done.3, bf16[48,9,192]{2,0,1:T(8,128)(2,1)} %collective-permute-done.2, bf16[48,9,192]{2,0,1:T(8,128)(2,1)} %collective-permute-done.1, f32[4,48,9,192]{3,1,2,0:T(8,128)} %get-tuple-element.17, s32[]{:T(128)S(6)} %select_n.28), kind=kLoop, calls=%fused_computation.10 | loop fusion | flops 497664 | bytes 1161220 | tf_op jit(solution)/shard_map/add | solution.py:338
  (26 shorter events, 0.2 us)
Async XLA Ops:
  0.6 27.2 %copy-start = (bf16[9,192,2,512]{3,2,1,0:T(2,128)(2,1)S(1)}, bf16[9,192,2,512]{3,2,1,0:T(2,128)(2,1)}, u32[]{:S(2)}) copy-start(bf16[9,192,2,512]{3,2,1,0:T(2,128)(2,1)} %param.8) | copy-start | bytes 10616836
  6.2 1.5 %copy-start.1 = (bf16[384,9,192]{2,0,1:T(8,128)(2,1)S(1)}, bf16[384,9,192]{2,0,1:T(8,128)(2,1)}, u32[]{:S(2)}) copy-start(bf16[384,9,192]{2,0,1:T(8,128)(2,1)} %copy.14) | copy-start | bytes 3981316
  7.7 1.0 copy-start.4
  24.7 0.9 copy-start.9
  25.7 1.3 %copy-start.7 = (bf16[2,2,2,192,512]{4,3,2,1,0:T(8,128)(2,1)}, bf16[2,2,2,192,512]{4,3,2,1,0:T(8,128)(2,1)S(1)}, u32[]{:S(2)}) copy-start(bf16[2,2,2,192,512]{4,3,2,1,0:T(8,128)(2,1)S(1)} %get-tuple-element.7.g_ref) | copy-start | bytes 4718596
  27.9 7.8 %copy-start.12 = (s32[2,16]{1,0:T(2,128)S(1)}, s32[2,16]{1,0:T(2,128)}, u32[]{:S(2)}) copy-start(s32[2,16]{1,0:T(2,128)} %param.11) | copy-start | bytes 388
  27.9 7.8 %copy-start.13 = (s32[2]{0:T(128)S(1)}, s32[2]{0:T(128)}, u32[]{:S(2)}) copy-start(s32[2]{0:T(128)} %param.13) | copy-start | bytes 28
  35.3 2.8 %collective-permute-start = (bf16[4,48,9,192]{3,1,2,0:T(8,128)(2,1)}, bf16[4,48,9,192]{3,1,2,0:T(8,128)(2,1)}, u32[]{:S(2)}, u32[]{:S(2)}) collective-permute-start(bf16[4,48,9,192]{3,1,2,0:T(8,128)(2,1)} %fusion.5), channel_id=1, source_target_pairs={{0,1},{1,0},{2,3},{3,2},{4,5},{5,4},{6,7},{7,6},{8,9},{9,8},{10,11... | collective-permute-start | bytes 1990664 | tf_op jit(solution)/shard_map/ppermute | solution.py:331
  35.8 11.1 %copy-start.8 = (bf16[2,2,2,192,512]{4,3,2,1,0:T(8,128)(2,1)S(1)}, bf16[2,2,2,192,512]{4,3,2,1,0:T(8,128)(2,1)}, u32[]{:S(2)}) copy-start(bf16[2,2,2,192,512]{4,3,2,1,0:T(8,128)(2,1)} %copy-done.7) | copy-start | bytes 4718596
  35.8 11.1 %copy-start.10 = (bf16[2,192,1152]{2,1,0:T(8,128)(2,1)S(1)}, bf16[2,192,1152]{2,1,0:T(8,128)(2,1)}, u32[]{:S(2)}) copy-start(bf16[2,192,1152]{2,1,0:T(8,128)(2,1)} %copy-done.9) | copy-start | bytes 2654212
  35.8 11.1 %copy-start.11 = (s32[2,16]{1,0:T(2,128)S(1)}, s32[2,16]{1,0:T(2,128)}, u32[]{:S(2)}) copy-start(s32[2,16]{1,0:T(2,128)} %shift.1) | copy-start | bytes 388
  42.2 56.1 %collective-permute-start.3 = (bf16[48,9,192]{2,0,1:T(8,128)(2,1)}, bf16[48,9,192]{2,0,1:T(8,128)(2,1)}, u32[]{:S(2)}, u32[]{:S(2)}) collective-permute-start(bf16[48,9,192]{2,0,1:T(8,128)(2,1)} %get-tuple-element.19), channel_id=1, source_target_pairs={{0,12},{4,0},{8,4},{12,8},{1,13},{5,1},{9,5},{13,9},{2,14},{6,2},{... | collective-permute-start | bytes 497672 | tf_op jit(solution)/shard_map/ppermute | solution.py:338
  45.8 52.5 %collective-permute-start.2 = (bf16[48,9,192]{2,0,1:T(8,128)(2,1)}, bf16[48,9,192]{2,0,1:T(8,128)(2,1)}, u32[]{:S(2)}, u32[]{:S(2)}) collective-permute-start(bf16[48,9,192]{2,0,1:T(8,128)(2,1)} %get-tuple-element.20), channel_id=1, source_target_pairs={{0,8},{4,12},{8,0},{12,4},{1,9},{5,13},{9,1},{13,5},{2,10},{6,14},... | collective-permute-start | bytes 497672 | tf_op jit(solution)/shard_map/ppermute | solution.py:338
  45.8 52.5 %collective-permute-start.1 = (bf16[48,9,192]{2,0,1:T(8,128)(2,1)}, bf16[48,9,192]{2,0,1:T(8,128)(2,1)}, u32[]{:S(2)}, u32[]{:S(2)}) collective-permute-start(bf16[48,9,192]{2,0,1:T(8,128)(2,1)} %get-tuple-element.18), channel_id=1, source_target_pairs={{0,4},{4,8},{8,12},{12,0},{1,5},{5,9},{9,13},{13,1},{2,6},{6,10},{... | collective-permute-start | bytes 497672 | tf_op jit(solution)/shard_map/ppermute | solution.py:338
  62.3 1.2 %copy-start.2 = (bf16[4,2,2,96,512]{4,3,2,1,0:T(8,128)(2,1)}, bf16[4,2,2,96,512]{4,3,2,1,0:T(8,128)(2,1)S(1)}, u32[]{:S(2)}) copy-start(bf16[4,2,2,96,512]{4,3,2,1,0:T(8,128)(2,1)S(1)} %get-tuple-element.10.far_ref) | copy-start | bytes 4718596
  63.4 0.9 copy-start.5
  64.3 1.4 %copy-start.3 = (bf16[4,2,2,96,512]{4,3,2,1,0:T(8,128)(2,1)S(1)}, bf16[4,2,2,96,512]{4,3,2,1,0:T(8,128)(2,1)}, u32[]{:S(2)}) copy-start(bf16[4,2,2,96,512]{4,3,2,1,0:T(8,128)(2,1)} %copy-done.2) | copy-start | bytes 4718596
  65.7 1.1 %copy-start.6 = (f32[2,2,96,512]{3,2,1,0:T(8,128)S(1)}, f32[2,2,96,512]{3,2,1,0:T(8,128)}, u32[]{:S(2)}) copy-start(f32[2,2,96,512]{3,2,1,0:T(8,128)} %copy-done.5) | copy-start | bytes 2359300

commit v3 on v2

v3 whole, which is shorter than its diff:
```python
import functools

import jax
import jax.numpy as jnp
from jax import lax
from jax.experimental import pallas as pl
from jax.experimental.pallas import tpu as pltpu
from jax.sharding import PartitionSpec as P

HALO_DEV = 2
BLOCK = 64
LANES = 128


MESH = pl.DeviceIdType.MESH
ROOM = 48 * 1024 * 1024


def gather_kernel(g_ref, q_hbm, whole, t_ref, q_ref, fetch, out_sem, in_sem):
    groups = lax.axis_size("ch")
    ch, lon = lax.axis_index("ch"), lax.axis_index("lon")
    rows, entries, basis = q_ref.shape[0], q_ref.shape[1], q_ref.shape[2]
    tiles = pltpu.make_async_copy(q_hbm, q_ref, fetch.at[0])
    tiles.start()
    barrier = pltpu.get_barrier_semaphore()
    for step in range(1, groups):
        pl.semaphore_signal(
            barrier, inc=1, device_id={"ch": lax.rem(ch + step, groups)}, device_id_type=MESH
        )
    pl.semaphore_signal(barrier, inc=1, device_id={"lon": 1 - lon}, device_id_type=MESH)
    pl.semaphore_wait(barrier, groups)

    across = [
        pltpu.make_async_remote_copy(
            src_ref=g_ref,
            dst_ref=whole.at[0, ch],
            send_sem=out_sem.at[step],
            recv_sem=in_sem.at[step],
            device_id={"ch": lax.rem(ch + step, groups)},
            device_id_type=MESH,
        )
        for step in range(1, groups)
    ]
    for copy in across:
        copy.start()

    def beside(step):
        source = lax.rem(ch + groups - step, groups)
        return pltpu.make_async_remote_copy(
            src_ref=g_ref if step == 0 else whole.at[0, source],
            dst_ref=whole.at[1, source],
            send_sem=out_sem.at[groups + step],
            recv_sem=in_sem.at[groups + step],
            device_id={"lon": 1 - lon},
            device_id_type=MESH,
        )

    forward = [beside(step) for step in range(groups)]
    forward[0].start()
    whole[0, ch] = g_ref[...]

    tiles.wait()
    for row in range(rows):

        @pl.loop(0, entries // 2)
        def _(pair):
            two = jnp.concatenate(
                [
                    q_ref[row, 2 * pair].reshape(basis * BLOCK, BLOCK),
                    q_ref[row, 2 * pair + 1].reshape(basis * BLOCK, BLOCK),
                ],
                axis=1,
            )
            t_ref[row, pl.ds(pl.multiple_of(pair * 2 * BLOCK, 2 * BLOCK), 2 * BLOCK)] = two.T

    for step in range(1, groups):
        across[step - 1].wait_recv()
        forward[step].start()
    for copy in across:
        copy.wait_send()
    for copy in forward:
        copy.wait()


def gathered(turned_out, quad_tiles):
    rows, channels, width = turned_out.shape
    entries, basis = quad_tiles.shape[1:3]
    groups = lax.axis_size("ch")
    vmem = pl.BlockSpec(memory_space=pltpu.VMEM)
    far = pl.BlockSpec(memory_space=pl.ANY)
    return pl.pallas_call(
        gather_kernel,
        out_shape=(
            jax.ShapeDtypeStruct((2, groups, rows, channels, width), jnp.bfloat16),
            jax.ShapeDtypeStruct((rows, entries * BLOCK, basis * BLOCK), jnp.bfloat16),
        ),
        in_specs=[vmem, far],
        out_specs=(vmem, vmem),
        scratch_shapes=[
            pltpu.VMEM(quad_tiles.shape, jnp.bfloat16),
            pltpu.SemaphoreType.DMA((1,)),
            pltpu.SemaphoreType.DMA((2 * groups,)),
            pltpu.SemaphoreType.DMA((2 * groups,)),
        ],
        compiler_params=pltpu.CompilerParams(
            collective_id=0, has_side_effects=True, vmem_limit_bytes=ROOM
        ),
        cost_estimate=pl.CostEstimate(flops=0, bytes_accessed=10 * 2**20, transcendentals=0),
    )(turned_out, quad_tiles)


def sum_kernel(
    far_hbm, near_hbm, out_ref, own, relay, arrived, near, beside, fetch, relay_sem, row_sem, pair_sem
):
    lat_devices = lax.axis_size("lat")
    lat, lon = lax.axis_index("lat"), lax.axis_index("lon")
    rows, own_half = near.shape[:2]
    offsets = [step for step in range(-HALO_DEV, HALO_DEV + 1) if step != 0]
    ways = (1, -1)
    parts = [(way, side, row) for side in range(2) for row in range(rows) for way in range(2)]

    def reaches(step):
        return jnp.logical_and(lat + step >= 0, lat + step < lat_devices)

    loads = [pltpu.make_async_copy(near_hbm.at[0], near, fetch.at[2])]
    for way, step in enumerate(ways):
        loads.append(
            pltpu.make_async_copy(far_hbm.at[offsets.index(step)], own.at[way], fetch.at[way])
        )
    for load in loads:
        load.start()

    barrier = pltpu.get_barrier_semaphore()
    pl.semaphore_signal(barrier, inc=1, device_id={"lon": 1 - lon}, device_id_type=MESH)
    for step in ways:

        @pl.when(reaches(step))
        def _():
            for side in range(2):
                pl.semaphore_signal(
                    barrier,
                    inc=1,
                    device_id={"lat": lat + step, "lon": lax.rem(lon + side, 2)},
                    device_id_type=MESH,
                )

    pl.semaphore_wait(barrier, 1 + sum(jnp.where(reaches(step), 2, 0) for step in ways))

    def passed(way, side, row):
        return pltpu.make_async_remote_copy(
            src_ref=far_hbm.at[offsets.index(2 * ways[way]), side, row],
            dst_ref=relay.at[way, side, row],
            send_sem=relay_sem.at[0, way, side, row],
            recv_sem=relay_sem.at[1, way, side, row],
            device_id={"lat": lat + ways[way]},
            device_id_type=MESH,
        )

    def message(way, side, row):
        return pltpu.make_async_remote_copy(
            src_ref=own.at[way, side, row],
            dst_ref=arrived.at[way, side, row],
            send_sem=row_sem.at[0, way, side, row],
            recv_sem=row_sem.at[1, way, side, row],
            device_id={"lat": lat + ways[way], "lon": lax.rem(lon + side, 2)},
            device_id_type=MESH,
        )

    pair = pltpu.make_async_remote_copy(
        src_ref=near_hbm.at[1],
        dst_ref=beside,
        send_sem=pair_sem.at[0],
        recv_sem=pair_sem.at[1],
        device_id={"lon": 1 - lon},
        device_id_type=MESH,
    )
    for part in parts:

        @pl.when(reaches(2 * ways[part[0]]))
        def _():
            passed(*part).start()

    pair.start()
    spans = [
        pl.ds(pl.multiple_of(lax.rem(lon + side, 2) * own_half, 8), own_half) for side in range(2)
    ]
    for load in loads:
        load.wait()
    out_ref[:, spans[0]] = near[...]
    for part in parts:
        step = ways[part[0]]

        @pl.when(jnp.logical_and(reaches(step), reaches(-step)))
        def _():
            passed(*part).wait_recv()
            total = own[part].astype(jnp.float32) + relay[part].astype(jnp.float32)
            own[part] = total.astype(jnp.bfloat16)

        @pl.when(reaches(step))
        def _():
            message(*part).start()

    pair.wait_recv()
    out_ref[:, spans[1]] = beside[...]
    for part in parts:

        @pl.when(reaches(-ways[part[0]]))
        def _():
            message(*part).wait_recv()
            out_ref[part[2], spans[part[1]]] += arrived[part].astype(jnp.float32)

    pair.wait_send()
    for part in parts:
        step = ways[part[0]]

        @pl.when(reaches(2 * step))
        def _():
            passed(*part).wait_send()

        @pl.when(reaches(step))
        def _():
            message(*part).wait_send()


def summed(far, near):
    _, rows, own_half, width = near.shape
    either = pl.BlockSpec(memory_space=pl.ANY)
    return pl.pallas_call(
        sum_kernel,
        out_shape=jax.ShapeDtypeStruct((rows, 2 * own_half, width), jnp.float32),
        in_specs=[either, either],
        out_specs=pl.BlockSpec(memory_space=pltpu.VMEM),
        scratch_shapes=[
            *[pltpu.VMEM((2, 2, rows, own_half, width), jnp.bfloat16)] * 3,
            *[pltpu.VMEM((rows, own_half, width), jnp.float32)] * 2,
            pltpu.SemaphoreType.DMA((3,)),
            pltpu.SemaphoreType.DMA((2, 2, 2, rows)),
            pltpu.SemaphoreType.DMA((2, 2, 2, rows)),
            pltpu.SemaphoreType.DMA((2,)),
        ],
        compiler_params=pltpu.CompilerParams(
            collective_id=1, has_side_effects=True, vmem_limit_bytes=ROOM
        ),
        cost_estimate=pl.CostEstimate(flops=0, bytes_accessed=40 * 2**20, transcendentals=0),
    )(far, near)


def quadrature_kernel(
    own_half,
    target,
    shift,
    lon,
    g_ref,
    k_ref,
    t_ref,
    far_hbm,
    near_hbm,
    far_ref,
    near_ref,
    w_ref,
    acc,
    mixed,
    piece,
    store,
):
    lon_halves, groups, rows, channels, width = g_ref.shape
    window, cycle_blocks = acc.shape[0] - 1, acc.shape[1]
    entries = target.shape[1]
    basis = k_ref.shape[0]
    blocks = width // BLOCK
    pairs = cycle_blocks // 2
    acc[...] = jnp.zeros_like(acc)
    w_ref[...] = jnp.zeros_like(w_ref)
    for half in range(2):

        @pl.when(lon[0] == half)
        def _():
            for k in range(basis):
                for group in range(groups):
                    w_ref[group, :, k * LANES : k * LANES + own_half] = k_ref[
                        k,
                        group * channels : (group + 1) * channels,
                        half * own_half : (half + 1) * own_half,
                    ]

    for row in range(rows):
        for half in range(lon_halves):
            total = None
            for group in range(groups):
                term = lax.dot_general(
                    g_ref[half, group, row],
                    w_ref[group],
                    (((0,), (0,)), ((), ())),
                    preferred_element_type=jnp.float32,
                )
                total = term if total is None else total + term
            total = total.astype(jnp.bfloat16)
            first = lax.rem(lon[0] + half, 2) * (blocks // 2)
            for block in range(blocks):
                for k in range(basis):
                    mixed[
                        first + block // 2,
                        k * BLOCK : (k + 1) * BLOCK,
                        (block % 2) * LANES : (block % 2 + 1) * LANES,
                    ] = total[block * BLOCK : (block + 1) * BLOCK, k * LANES : (k + 1) * LANES]

        @pl.loop(0, pairs)
        def _(pair):
            piece[...] = jnp.dot(
                t_ref[row], mixed[pair], preferred_element_type=jnp.float32
            )
            for entry in range(entries):
                for side in range(2):
                    place = lax.rem(2 * pair + side + shift[row, entry], cycle_blocks)
                    acc[target[row, entry], place] += piece[
                        entry * BLOCK : (entry + 1) * BLOCK, side * LANES : (side + 1) * LANES
                    ]

    steps = window // rows
    mid = steps // 2
    saves = []
    for step in sorted(range(steps), key=lambda at: -abs(at - mid)):
        far = step - (step > mid)
        for side in range(2):
            half = lax.rem(lon[0] + side, 2)
            for row in range(rows):
                block = acc[step * rows + row, pl.ds(half * blocks, blocks)]
                turned = block.reshape(width, LANES).T[:own_half]
                if step == mid:
                    near_ref[side, row] = turned
                else:
                    far_ref[far, side, row] = turned.astype(jnp.bfloat16)
            if step == mid:
                save = pltpu.make_async_copy(near_ref.at[side], near_hbm.at[side], store.at[step, side])
            else:
                save = pltpu.make_async_copy(
                    far_ref.at[far, side], far_hbm.at[far, side], store.at[step, side]
                )
            save.start()
            saves.append(save)
    for save in saves:
        save.wait()


def quadrature(own_half, target, shift, lon, g, w, t, window):
    lon_halves, groups, rows, channels, width = g.shape
    cycle_blocks = lon_halves * width // BLOCK
    depth = t.shape[2]
    vmem = pl.BlockSpec(memory_space=pltpu.VMEM)
    smem = pl.BlockSpec(memory_space=pltpu.SMEM)
    return pl.pallas_call(
        functools.partial(quadrature_kernel, own_half),
        out_shape=(
            jax.ShapeDtypeStruct(
                (window // rows - 1, 2, rows, own_half, width), jnp.bfloat16
            ),
            jax.ShapeDtypeStruct((2, rows, own_half, width), jnp.float32),
        ),
        in_specs=[smem, smem, smem, vmem, vmem, vmem],
        out_specs=(pl.BlockSpec(memory_space=pl.ANY), pl.BlockSpec(memory_space=pl.ANY)),
        scratch_shapes=[
            pltpu.VMEM((window // rows - 1, 2, rows, own_half, width), jnp.bfloat16),
            pltpu.VMEM((2, rows, own_half, width), jnp.float32),
            pltpu.VMEM((groups, channels, w.shape[0] * LANES), jnp.bfloat16),
            pltpu.VMEM((window + 1, cycle_blocks, BLOCK, LANES), jnp.float32),
            pltpu.VMEM((cycle_blocks // 2, depth, 2 * LANES), jnp.bfloat16),
            pltpu.VMEM((t.shape[1], 2 * LANES), jnp.float32),
            pltpu.SemaphoreType.DMA((window // rows, 2)),
        ],
        compiler_params=pltpu.CompilerParams(vmem_limit_bytes=ROOM),
        cost_estimate=pl.CostEstimate(
            flops=9 * 10**9, bytes_accessed=10 * 2**20, transcendentals=0
        ),
    )(target, shift, lon, g, w, t)


def filter_gradient(full_out, saved_basis):
    groups, rows, channels, width = full_out.shape
    basis = saved_basis.shape[0]
    lat_devices = lax.axis_size("lat")
    lon_devices = lax.axis_size("lon")
    own_rows = groups * channels // (lat_devices * lon_devices)
    if lat_devices > 8 or lon_devices != 2 or channels % (2 * own_rows):
        product = jnp.einsum(
            "crow,kirw->coki", full_out, saved_basis, preferred_element_type=jnp.float32
        )
        return lax.psum_scatter(
            product.reshape(groups * channels, basis, channels),
            ("lat", "lon"),
            scatter_dimension=0,
            tiled=True,
        )
    lat = lax.axis_index("lat")
    lon = lax.axis_index("lon")
    split = full_out.reshape(groups, rows, channels // (2 * own_rows), 2, own_rows, width)

    def half(which):
        product = jnp.einsum(
            "crlow,kirw->cloki",
            lax.dynamic_index_in_dim(split, which, 3, keepdims=False),
            saved_basis,
            preferred_element_type=jnp.float32,
        )
        return product.reshape(lat_devices, own_rows, basis, channels)

    received = lax.ppermute(half(1 - lon).astype(jnp.bfloat16), "lon", [(0, 1), (1, 0)])
    kept = half(lon)

    def both(step):
        at = lax.rem(lat + step, lat_devices)
        mine = lax.dynamic_index_in_dim(kept, at, 0, keepdims=False)
        return mine + lax.dynamic_index_in_dim(received, at, 0, keepdims=False)

    result = both(0)
    for step in range(1, lat_devices):
        result = result + lax.ppermute(
            both(step).astype(jnp.bfloat16),
            "lat",
            [(at, (at + step) % lat_devices) for at in range(lat_devices)],
        )
    return result


def body(grad_out, saved_basis, weight, quad_tiles, col_rows, col_shift, block_count):
    channels, rows, width = grad_out.shape
    entries = quad_tiles.shape[1]
    lat = lax.axis_index("lat")
    lon = lax.axis_index("lon")
    own_half = channels // 2
    window = (2 * HALO_DEV + 1) * rows

    whole_out, turned = gathered(grad_out.transpose(1, 0, 2), quad_tiles)
    grad_weight = filter_gradient(whole_out[0], saved_basis)
    live = jnp.arange(entries, dtype=jnp.int32)[None, :] < block_count[:, None]
    target = jnp.where(live, col_rows - (lat - HALO_DEV) * rows, window)
    far, near = quadrature(
        own_half, target, col_shift, lon[None].astype(jnp.int32), whole_out, weight.transpose(1, 0, 2), turned, window
    )

    grad_input = summed(far, near).transpose(1, 0, 2)
    return (grad_input, grad_weight)


def solution(mesh):
    in_specs = (
        P("ch", ("grp", "lat"), "lon"),
        P(None, "ch", ("grp", "lat"), "lon"),
        P(None, None, "ch"),
        P("lat", None, None, None, None),
        P("lat", None),
        P("lat", None),
        P("lat"),
    )
    out_specs = (P("ch", ("grp", "lat"), "lon"), P(("grp", "lat", "lon"), None, "ch"))
    return jax.shard_map(body, mesh=mesh, in_specs=in_specs, out_specs=out_specs, check_vma=False)
```

time: 101 us -> 80.7 us (0.80)
  local copies, waits for them, and re-layouts: 20.6 us -> 8.27 us
  Pallas kernels: 61.4 us -> 53.9 us
  matrix products: 4.94 us -> 7.37 us
  waiting for transfers between devices: 2.32 us -> 0.01 us
    pallas_call x1, Pallas kernels: 30 us -> 20.8 us  [summed(): pl.pallas_call(sum_kernel, out_shape=jax.ShapeDtypeStruct((rows, 2 * own_...]
    unnamed x31 -> x23, local copies, waits for them, and re-layouts: 16.3 us -> 8.11 us
    pallas_call x1, Pallas kernels: 15.4 us -> 18.9 us  [quadrature(): pl.pallas_call(functools.partial(quadrature_kernel, own_half), out_shape=...]
    convert_element_type x1 -> x0, local copies, waits for them, and re-layouts: 2.52 us -> none  [filter_gradient(): given.astype(jnp.bfloat16)]
    dot_general x1 -> x2, matrix products: 4.94 us -> 7.37 us  [half(): jnp.einsum('crlow,kirw->cloki', lax.dynamic_index_in_dim(split, which, 3,...]
    ppermute x4, waiting for transfers between devices: 2.32 us -> 0.01 us  [the longest x3 0.01 us: filter_gradient(): lax.ppermute(both(step).astype(jnp.bfloat16), 'lat', [(at, (at + step) %...]
    pallas_call x1, Pallas kernels: 16 us -> 14.2 us  [gathered(): pl.pallas_call(gather_kernel, out_shape=(jax.ShapeDtypeStruct((2, groups,...]
  transfers between devices with their start and end apart: 4 -> 4, of which waited for: 1 -> 0; matrix products, arithmetic and copies ran while one was open for 2% -> 7% of each run, Pallas kernels for 45% -> 49%
where the time goes in v3:
time: 80.7 us; the launch traced here: 80.4 us
  Pallas kernels  53.9 us (67%)
  local copies, waits for them, and re-layouts  8.27 us (10%)
  matrix products  7.37 us (9%)
  other arithmetic  5.01 us (6%)
  starting transfers between devices  4.98 us (6%)
    pallas_call x1, Pallas kernels, summed(): pl.pallas_call(sum_kernel, out_shape=jax.ShapeDtypeStruct((rows, 2 * own_...  20.8 us
    pallas_call x1, Pallas kernels, quadrature(): pl.pallas_call(functools.partial(quadrature_kernel, own_half), out_shape=...  18.9 us
    pallas_call x1, Pallas kernels, gathered(): pl.pallas_call(gather_kernel, out_shape=(jax.ShapeDtypeStruct((2, groups,...  14.2 us
    unnamed x23, local copies, waits for them, and re-layouts  8.11 us
    dot_general x2, matrix products, half(): jnp.einsum('crlow,kirw->cloki', lax.dynamic_index_in_dim(split, which, 3,...  7.37 us
    ppermute x3, starting transfers between devices, filter_gradient(): lax.ppermute(both(step).astype(jnp.bfloat16), 'lat', [(at, (at + step) %...  4.6 us
    convert_element_type x1, other arithmetic, filter_gradient(): both(step).astype(jnp.bfloat16)  2.73 us
    add x1, other arithmetic, filter_gradient(): result + lax.ppermute(both(step).astype(jnp.bfloat16), 'lat', [(at, (at +...  2.21 us
  transfers between devices with their start and end apart: 4, of which 0 were waited for; matrix products, arithmetic and copies ran while one was open for 7% of the time, Pallas kernels for 49%

profile of v3, /device:TPU:0, one launch (start us, length us, event | category | flops | bytes accessed | tf_op | source)
XLA Modules:
  0.0 80.4 jit_solution(8042265282803458702)
XLA Ops:
  0.6 1.0 %copy.42 = bf16[192,2,512]{2,0,1:T(8,128)(2,1)S(1)} copy(bf16[192,2,512]{2,1,0:T(2,128)(2,1)} %param.7) | data formatting | bytes 786432 | tf_op args[0]
  1.7 14.2 %shard_map.86 = (bf16[2,2,2,192,512]{4,3,2,1,0:T(8,128)(2,1)S(1)}, bf16[2,1024,576]{2,1,0:T(8,128)(2,1)S(1)}) custom-call(bf16[2,192,512]{2,1,0:T(8,128)(2,1)S(1)} %bitcast.61, bf16[2,16,9,64,64]{4,3,2,1,0:T(8,128)(2,1)} %q_hbm.1), custom_call_target="tpu_custom_call" | custom-call | bytes 10485760 | tf_op jit(solution)/shard_map/pallas_call | solution.py:91
  15.9 1.5 %copy-done.4 = bf16[2,1024,576]{2,1,0:T(8,128)(2,1)} copy-done((bf16[2,1024,576]{2,1,0:T(8,128)(2,1)}, bf16[2,1024,576]{2,1,0:T(8,128)(2,1)S(1)}, u32[]{:S(2)}) %copy-start.4) | copy-done | bytes 2359320
  17.4 0.1 slice.3
  17.4 1.2 %copy-done.2 = bf16[2,2,2,192,512]{4,3,2,1,0:T(8,128)(2,1)} copy-done((bf16[2,2,2,192,512]{4,3,2,1,0:T(8,128)(2,1)}, bf16[2,2,2,192,512]{4,3,2,1,0:T(8,128)(2,1)S(1)}, u32[]{:S(2)}) %copy-start.2) | copy-done | bytes 1572888
  18.6 0.1 dynamic-slice_bitcast_fusion
  18.7 0.0 copy-start.7
  18.7 4.1 %bitcast_convert_fusion = bf16[4,48,9,192]{3,1,2,0:T(8,128)(2,1)} fusion(bf16[4,48,2,512,1]{3,1,2,4,0:T(8,128)(2,1)S(1)} %bitcast.64, bf16[9,192,2,512]{3,2,1,0:T(2,128)(2,1)} %param.8), kind=kOutput, calls=%fused_computation.6 | convolution fusion | flops 679809024 | bytes 4595712 | tf_op jit(solution)/shard_map/crlow,kirw->cloki/dot_general | solution.py:398
  22.9 0.4 collective-permute-start
  23.2 0.9 %copy.15 = bf16[384,9,192]{2,0,1:T(8,128)(2,1)S(1)} copy(bf16[384,9,192]{0,2,1:T(8,128)(2,1)S(1)} %copy-done.7) | data formatting | bytes 2654208 | tf_op args[2]
  24.2 0.1 compare_select_fusion.target
  24.3 3.2 %fusion.6 = f32[4,48,9,192]{3,1,2,0:T(8,128)S(1)} fusion(bf16[4,48,2,512,1]{3,1,2,4,0:T(8,128)(2,1)S(1)} %bitcast.63, bf16[9,192,2,512]{3,2,1,0:T(2,128)(2,1)} %param.8), kind=kOutput, calls=%fused_computation.7 | convolution fusion | flops 679477248 | bytes 5259264 | tf_op jit(solution)/shard_map/crlow,kirw->cloki/dot_general | solution.py:398
  27.5 0.0 collective-permute-done
  27.6 2.7 %fusion.13 = (bf16[48,9,192]{2,0,1:T(8,128)(2,1)}, bf16[48,9,192]{2,0,1:T(8,128)(2,1)}, bf16[48,9,192]{2,0,1:T(8,128)(2,1)}) fusion(f32[4,48,9,192]{3,1,2,0:T(8,128)S(1)} %fusion.6, s32[]{:T(128)S(6)} %select_n.33, bf16[4,48,9,192]{3,1,2,0:T(8,128)(2,1)} %collective-permute-done, s32[]{:T(128)S(6)} %select_n.35, s32[]{:T(128)S(6)} %select_n.34), kind=kLoop, calls=%fused_computation.17 | loop fusion | flops 746496 | bytes 1990668 | tf_op jit(solution)/shard_map/convert_element_type | solution.py:417
  30.3 3.6 %collective-permute-start.3 = (bf16[48,9,192]{2,0,1:T(8,128)(2,1)}, bf16[48,9,192]{2,0,1:T(8,128)(2,1)}, u32[]{:S(2)}, u32[]{:S(2)}) collective-permute-start(bf16[48,9,192]{2,0,1:T(8,128)(2,1)} %get-tuple-element.15), channel_id=1, source_target_pairs={{0,12},{4,0},{8,4},{12,8},{1,13},{5,1},{9,5},{13,9},{2,14},{6,2},{... | collective-permute-start | bytes 497672 | tf_op jit(solution)/shard_map/ppermute | solution.py:416
  33.9 0.0 collective-permute-start.2
  33.9 1.0 %collective-permute-start.1 = (bf16[48,9,192]{2,0,1:T(8,128)(2,1)}, bf16[48,9,192]{2,0,1:T(8,128)(2,1)}, u32[]{:S(2)}, u32[]{:S(2)}) collective-permute-start(bf16[48,9,192]{2,0,1:T(8,128)(2,1)} %get-tuple-element.14), channel_id=1, source_target_pairs={{0,4},{4,8},{8,12},{12,0},{1,5},{5,9},{9,13},{13,1},{2,6},{6,10},{... | collective-permute-start | bytes 497672 | tf_op jit(solution)/shard_map/ppermute | solution.py:416
  34.9 18.9 %shard_map.87 = (bf16[4,2,2,96,512]{4,3,2,1,0:T(8,128)(2,1)S(1)}, f32[2,2,96,512]{3,2,1,0:T(8,128)S(1)}) custom-call(s32[2,16]{1,0:T(2,128)S(1)} %compare_select_fusion.target, s32[2,16]{1,0:T(2,128)S(1)} %copy-done.5, s32[1]{0:T(128)} %bitcast.lon, bf16[2,2,2,192,512]{4,3,2,1,0:T(8,128)(2,1)S(1)} %copy-done.3, bf16[9,384,192]{2,1,0:T(8,128)(2,1)S(1)} %bitcast.60, ...), custom_call_target="tpu_custom_call" | custom-call | flops 8999999488 | bytes 10485760 | tf_op jit(solution)/shard_map/pallas_call | solution.py:351
  53.8 0.0 copy-start
  53.8 0.9 %copy-done = f32[2,2,96,512]{3,2,1,0:T(8,128)} copy-done((f32[2,2,96,512]{3,2,1,0:T(8,128)}, f32[2,2,96,512]{3,2,1,0:T(8,128)S(1)}, u32[]{:S(2)}) %copy-start) | copy-done | bytes 786456
  54.7 1.1 %copy-done.1 = f32[2,2,96,512]{3,2,1,0:T(8,128)S(1)} copy-done((f32[2,2,96,512]{3,2,1,0:T(8,128)S(1)}, f32[2,2,96,512]{3,2,1,0:T(8,128)}, u32[]{:S(2)}) %copy-start.1) | copy-done | bytes 786456
  55.8 20.8 %shard_map.88 = f32[2,192,512]{2,1,0:T(8,128)S(1)} custom-call(bf16[4,2,2,96,512]{4,3,2,1,0:T(8,128)(2,1)S(1)} %get-tuple-element.8.far_hbm, f32[2,2,96,512]{3,2,1,0:T(8,128)S(1)} %copy-done.1), custom_call_target="tpu_custom_call" | custom-call | bytes 41943040 | tf_op jit(solution)/shard_map/pallas_call | solution.py:228
  76.7 1.5 %copy.22 = f32[192,2,512]{2,1,0:T(2,128)} copy(f32[192,2,512]{2,0,1:T(8,128)S(1)} %bitcast.59) | data formatting | bytes 1572864
  78.2 2.2 %fusion.12 = f32[48,9,192]{2,0,1:T(8,128)} fusion(bf16[48,9,192]{2,0,1:T(8,128)(2,1)} %collective-permute-done.3, bf16[48,9,192]{2,0,1:T(8,128)(2,1)} %collective-permute-done.2, bf16[48,9,192]{2,0,1:T(8,128)(2,1)} %collective-permute-done.1, f32[4,48,9,192]{3,1,2,0:T(8,128)} %copy-done.6, s32[]{:T(128)S(6)} %select_n.31, ...), kind=kLoop, calls=%fused_computation.10 | loop fusion | flops 663552 | bytes 1327108 | tf_op jit(solution)/shard_map/add | solution.py:416
  (19 shorter events, 0.1 us)
Async XLA Ops:
  15.9 1.5 %copy-start.4 = (bf16[2,1024,576]{2,1,0:T(8,128)(2,1)}, bf16[2,1024,576]{2,1,0:T(8,128)(2,1)S(1)}, u32[]{:S(2)}) copy-start(bf16[2,1024,576]{2,1,0:T(8,128)(2,1)S(1)} %get-tuple-element.7.t_ref) | copy-start | bytes 7077892
  17.4 1.2 %copy-start.2 = (bf16[2,2,2,192,512]{4,3,2,1,0:T(8,128)(2,1)}, bf16[2,2,2,192,512]{4,3,2,1,0:T(8,128)(2,1)S(1)}, u32[]{:S(2)}) copy-start(bf16[2,2,2,192,512]{4,3,2,1,0:T(8,128)(2,1)S(1)} %get-tuple-element.6.g_ref) | copy-start | bytes 4718596
  18.7 4.5 %copy-start.7 = (bf16[384,9,192]{0,2,1:T(8,128)(2,1)S(1)}, bf16[384,9,192]{0,2,1:T(8,128)(2,1)}, u32[]{:S(2)}) copy-start(bf16[384,9,192]{0,2,1:T(8,128)(2,1)} %param.9) | copy-start | bytes 3981316
  22.9 1.3 %copy-start.8 = (s32[2,16]{1,0:T(2,128)S(1)}, s32[2,16]{1,0:T(2,128)}, u32[]{:S(2)}) copy-start(s32[2,16]{1,0:T(2,128)} %param.11) | copy-start | bytes 388
  22.9 1.3 %copy-start.9 = (s32[2]{0:T(128)S(1)}, s32[2]{0:T(128)}, u32[]{:S(2)}) copy-start(s32[2]{0:T(128)} %param.13) | copy-start | bytes 28
  22.9 4.7 %collective-permute-start = (bf16[4,48,9,192]{3,1,2,0:T(8,128)(2,1)}, bf16[4,48,9,192]{3,1,2,0:T(8,128)(2,1)}, u32[]{:S(2)}, u32[]{:S(2)}) collective-permute-start(bf16[4,48,9,192]{3,1,2,0:T(8,128)(2,1)} %bitcast_convert_fusion), channel_id=1, source_target_pairs={{0,1},{1,0},{2,3},{3,2},{4,5},{5,4},{6,7},{7,6},{8,9},{9,8},{10,11... | collective-permute-start | bytes 1990664 | tf_op jit(solution)/shard_map/ppermute | solution.py:406
  24.3 10.6 %copy-start.3 = (bf16[2,2,2,192,512]{4,3,2,1,0:T(8,128)(2,1)S(1)}, bf16[2,2,2,192,512]{4,3,2,1,0:T(8,128)(2,1)}, u32[]{:S(2)}) copy-start(bf16[2,2,2,192,512]{4,3,2,1,0:T(8,128)(2,1)} %copy-done.2) | copy-start | bytes 4718596
  24.3 10.6 %copy-start.5 = (s32[2,16]{1,0:T(2,128)S(1)}, s32[2,16]{1,0:T(2,128)}, u32[]{:S(2)}) copy-start(s32[2,16]{1,0:T(2,128)} %shift.1) | copy-start | bytes 388
  27.5 7.4 %copy-start.6 = (f32[4,48,9,192]{3,1,2,0:T(8,128)}, f32[4,48,9,192]{3,1,2,0:T(8,128)S(1)}, u32[]{:S(2)}) copy-start(f32[4,48,9,192]{3,1,2,0:T(8,128)S(1)} %fusion.6) | copy-start | bytes 3981316
  30.3 47.9 %collective-permute-start.3 = (bf16[48,9,192]{2,0,1:T(8,128)(2,1)}, bf16[48,9,192]{2,0,1:T(8,128)(2,1)}, u32[]{:S(2)}, u32[]{:S(2)}) collective-permute-start(bf16[48,9,192]{2,0,1:T(8,128)(2,1)} %get-tuple-element.15), channel_id=1, source_target_pairs={{0,12},{4,0},{8,4},{12,8},{1,13},{5,1},{9,5},{13,9},{2,14},{6,2},{... | collective-permute-start | bytes 497672 | tf_op jit(solution)/shard_map/ppermute | solution.py:416
  33.9 44.3 %collective-permute-start.2 = (bf16[48,9,192]{2,0,1:T(8,128)(2,1)}, bf16[48,9,192]{2,0,1:T(8,128)(2,1)}, u32[]{:S(2)}, u32[]{:S(2)}) collective-permute-start(bf16[48,9,192]{2,0,1:T(8,128)(2,1)} %get-tuple-element.16), channel_id=1, source_target_pairs={{0,8},{4,12},{8,0},{12,4},{1,9},{5,13},{9,1},{13,5},{2,10},{6,14},... | collective-permute-start | bytes 497672 | tf_op jit(solution)/shard_map/ppermute | solution.py:416
  33.9 44.3 %collective-permute-start.1 = (bf16[48,9,192]{2,0,1:T(8,128)(2,1)}, bf16[48,9,192]{2,0,1:T(8,128)(2,1)}, u32[]{:S(2)}, u32[]{:S(2)}) collective-permute-start(bf16[48,9,192]{2,0,1:T(8,128)(2,1)} %get-tuple-element.14), channel_id=1, source_target_pairs={{0,4},{4,8},{8,12},{12,0},{1,5},{5,9},{9,13},{13,1},{2,6},{6,10},{... | collective-permute-start | bytes 497672 | tf_op jit(solution)/shard_map/ppermute | solution.py:416
  53.8 0.9 %copy-start = (f32[2,2,96,512]{3,2,1,0:T(8,128)}, f32[2,2,96,512]{3,2,1,0:T(8,128)S(1)}, u32[]{:S(2)}) copy-start(f32[2,2,96,512]{3,2,1,0:T(8,128)S(1)} %get-tuple-element.9.near_hbm) | copy-start | bytes 2359300
  54.7 1.1 %copy-start.1 = (f32[2,2,96,512]{3,2,1,0:T(8,128)S(1)}, f32[2,2,96,512]{3,2,1,0:T(8,128)}, u32[]{:S(2)}) copy-start(f32[2,2,96,512]{3,2,1,0:T(8,128)} %copy-done) | copy-start | bytes 2359300

commit v4 on v3

--- a/solution.py
+++ b/solution.py
@@ -13,7 +13,7 @@
 
 
 MESH = pl.DeviceIdType.MESH
-ROOM = 48 * 1024 * 1024
+MIB = 1024 * 1024
 
 
 def gather_kernel(g_ref, q_hbm, whole, t_ref, q_ref, fetch, out_sem, in_sem):
@@ -30,33 +30,32 @@
     pl.semaphore_signal(barrier, inc=1, device_id={"lon": 1 - lon}, device_id_type=MESH)
     pl.semaphore_wait(barrier, groups)
 
-    across = [
-        pltpu.make_async_remote_copy(
-            src_ref=g_ref,
-            dst_ref=whole.at[0, ch],
-            send_sem=out_sem.at[step],
-            recv_sem=in_sem.at[step],
+    def across(step, row):
+        return pltpu.make_async_remote_copy(
+            src_ref=g_ref.at[row],
+            dst_ref=whole.at[0, ch, row],
+            send_sem=out_sem.at[step, row],
+            recv_sem=in_sem.at[step, row],
             device_id={"ch": lax.rem(ch + step, groups)},
             device_id_type=MESH,
         )
-        for step in range(1, groups)
-    ]
-    for copy in across:
-        copy.start()
-
-    def beside(step):
+
+    def beside(step, row):
         source = lax.rem(ch + groups - step, groups)
         return pltpu.make_async_remote_copy(
-            src_ref=g_ref if step == 0 else whole.at[0, source],
-            dst_ref=whole.at[1, source],
-            send_sem=out_sem.at[groups + step],
-            recv_sem=in_sem.at[groups + step],
+            src_ref=g_ref.at[row] if step == 0 else whole.at[0, source, row],
+            dst_ref=whole.at[1, source, row],
+            send_sem=out_sem.at[groups + step, row],
+            recv_sem=in_sem.at[groups + step, row],
             device_id={"lon": 1 - lon},
             device_id_type=MESH,
         )
 
-    forward = [beside(step) for step in range(groups)]
-    forward[0].start()
+    for row in range(rows):
+        for step in range(1, groups):
+            across(step, row).start()
+    for row in range(rows):
+        beside(0, row).start()
     whole[0, ch] = g_ref[...]
 
     tiles.wait()
@@ -73,13 +72,15 @@
             )
             t_ref[row, pl.ds(pl.multiple_of(pair * 2 * BLOCK, 2 * BLOCK), 2 * BLOCK)] = two.T
 
-    for step in range(1, groups):
-        across[step - 1].wait_recv()
-        forward[step].start()
-    for copy in across:
-        copy.wait_send()
-    for copy in forward:
-        copy.wait()
+        for step in range(1, groups):
+            across(step, row).wait_recv()
+            beside(step, row).start()
+
+    for row in range(rows):
+        for step in range(1, groups):
+            across(step, row).wait_send()
+        for step in range(groups):
+            beside(step, row).wait()
 
 
 def gathered(turned_out, quad_tiles):
@@ -99,11 +100,11 @@
         scratch_shapes=[
             pltpu.VMEM(quad_tiles.shape, jnp.bfloat16),
             pltpu.SemaphoreType.DMA((1,)),
-            pltpu.SemaphoreType.DMA((2 * groups,)),
-            pltpu.SemaphoreType.DMA((2 * groups,)),
+            pltpu.SemaphoreType.DMA((2 * groups, rows)),
+            pltpu.SemaphoreType.DMA((2 * groups, rows)),
         ],
         compiler_params=pltpu.CompilerParams(
-            collective_id=0, has_side_effects=True, vmem_limit_bytes=ROOM
+            collective_id=0, has_side_effects=True, vmem_limit_bytes=20 * MIB
         ),
         cost_estimate=pl.CostEstimate(flops=0, bytes_accessed=10 * 2**20, transcendentals=0),
     )(turned_out, quad_tiles)
@@ -239,7 +240,7 @@
             pltpu.SemaphoreType.DMA((2,)),
         ],
         compiler_params=pltpu.CompilerParams(
-            collective_id=1, has_side_effects=True, vmem_limit_bytes=ROOM
+            collective_id=1, has_side_effects=True, vmem_limit_bytes=16 * MIB
         ),
         cost_estimate=pl.CostEstimate(flops=0, bytes_accessed=40 * 2**20, transcendentals=0),
     )(far, near)
@@ -304,17 +305,31 @@
                         (block % 2) * LANES : (block % 2 + 1) * LANES,
                     ] = total[block * BLOCK : (block + 1) * BLOCK, k * LANES : (k + 1) * LANES]
 
-        @pl.loop(0, pairs)
-        def _(pair):
-            piece[...] = jnp.dot(
-                t_ref[row], mixed[pair], preferred_element_type=jnp.float32
-            )
+        def multiply(pair, slot):
+            piece[slot] = jnp.dot(t_ref[row], mixed[pair], preferred_element_type=jnp.float32)
+
+        def put(pair, slot):
             for entry in range(entries):
                 for side in range(2):
                     place = lax.rem(2 * pair + side + shift[row, entry], cycle_blocks)
                     acc[target[row, entry], place] += piece[
-                        entry * BLOCK : (entry + 1) * BLOCK, side * LANES : (side + 1) * LANES
+                        slot,
+                        entry * BLOCK : (entry + 1) * BLOCK,
+                        side * LANES : (side + 1) * LANES,
                     ]
+
+        multiply(0, 0)
+
+        @pl.loop(0, pairs // 2 - 1)
+        def _(step):
+            multiply(2 * step + 1, 1)
+            put(2 * step, 0)
+            multiply(2 * step + 2, 0)
+            put(2 * step + 1, 1)
+
+        multiply(pairs - 1, 1)
+        put(pairs - 2, 0)
+        put(pairs - 1, 1)
 
     steps = window // rows
     mid = steps // 2
@@ -364,10 +379,10 @@
             pltpu.VMEM((groups, channels, w.shape[0] * LANES), jnp.bfloat16),
             pltpu.VMEM((window + 1, cycle_blocks, BLOCK, LANES), jnp.float32),
             pltpu.VMEM((cycle_blocks // 2, depth, 2 * LANES), jnp.bfloat16),
-            pltpu.VMEM((t.shape[1], 2 * LANES), jnp.float32),
+            pltpu.VMEM((2, t.shape[1], 2 * LANES), jnp.float32),
             pltpu.SemaphoreType.DMA((window // rows, 2)),
         ],
-        compiler_params=pltpu.CompilerParams(vmem_limit_bytes=ROOM),
+        compiler_params=pltpu.CompilerParams(vmem_limit_bytes=36 * MIB),
         cost_estimate=pl.CostEstimate(
             flops=9 * 10**9, bytes_accessed=10 * 2**20, transcendentals=0
         ),

time: 80.7 us -> 81.4 us (level)
  local copies, waits for them, and re-layouts: 8.27 us -> 10.6 us
  Pallas kernels: 53.9 us -> 52.3 us
    unnamed x23 -> x27, local copies, waits for them, and re-layouts: 8.11 us -> 10.4 us
    pallas_call x1, Pallas kernels: 18.9 us -> 17.2 us  [quadrature(): pl.pallas_call(functools.partial(quadrature_kernel, own_half), out_shape=...]
  transfers between devices with their start and end apart: 4 -> 4, of which waited for: 0 -> 0; matrix products, arithmetic and copies ran while one was open for 7% -> 7% of each run, Pallas kernels for 49% -> 47%
where the time goes in v4:
time: 81.4 us; the launch traced here: 81.1 us
  Pallas kernels  52.3 us (64%)
  local copies, waits for them, and re-layouts  10.6 us (13%)
  matrix products  7.4 us (9%)
  other arithmetic  5.03 us (6%)
  starting transfers between devices  4.99 us (6%)
    pallas_call x1, Pallas kernels, summed(): pl.pallas_call(sum_kernel, out_shape=jax.ShapeDtypeStruct((rows, 2 * own_...  20.8 us
    pallas_call x1, Pallas kernels, quadrature(): pl.pallas_call(functools.partial(quadrature_kernel, own_half), out_shape=...  17.2 us
    pallas_call x1, Pallas kernels, gathered(): pl.pallas_call(gather_kernel, out_shape=(jax.ShapeDtypeStruct((2, groups,...  14.3 us
    unnamed x27, local copies, waits for them, and re-layouts  10.4 us
    dot_general x2, matrix products, half(): jnp.einsum('crlow,kirw->cloki', lax.dynamic_index_in_dim(split, which, 3,...  7.4 us
    ppermute x3, starting transfers between devices, filter_gradient(): lax.ppermute(both(step).astype(jnp.bfloat16), 'lat', [(at, (at + step) %...  4.62 us
    convert_element_type x1, other arithmetic, filter_gradient(): both(step).astype(jnp.bfloat16)  2.75 us
    add x1, other arithmetic, filter_gradient(): result + lax.ppermute(both(step).astype(jnp.bfloat16), 'lat', [(at, (at +...  2.21 us
  transfers between devices with their start and end apart: 4, of which 0 were waited for; matrix products, arithmetic and copies ran while one was open for 7% of the time, Pallas kernels for 47%

profile of v4, /device:TPU:0, one launch (start us, length us, event | category | flops | bytes accessed | tf_op | source)
XLA Modules:
  0.0 81.1 jit_solution(7157695188913035668)
XLA Ops:
  0.6 1.0 %copy.42 = bf16[192,2,512]{2,0,1:T(8,128)(2,1)S(1)} copy(bf16[192,2,512]{2,1,0:T(2,128)(2,1)} %param.7) | data formatting | bytes 786432 | tf_op args[0]
  1.7 0.0 copy-start
  1.7 2.3 %copy-done = bf16[2,16,9,64,64]{4,3,2,1,0:T(8,128)(2,1)S(1)} copy-done((bf16[2,16,9,64,64]{4,3,2,1,0:T(8,128)(2,1)S(1)}, bf16[2,16,9,64,64]{4,3,2,1,0:T(8,128)(2,1)}, u32[]{:S(2)}) %copy-start) | copy-done | bytes 2359320
  4.0 14.3 %shard_map.86 = (bf16[2,2,2,192,512]{4,3,2,1,0:T(8,128)(2,1)S(1)}, bf16[2,1024,576]{2,1,0:T(8,128)(2,1)S(1)}) custom-call(bf16[2,192,512]{2,1,0:T(8,128)(2,1)S(1)} %bitcast.61, bf16[2,16,9,64,64]{4,3,2,1,0:T(8,128)(2,1)S(1)} %copy-done), custom_call_target="tpu_custom_call" | custom-call | bytes 10485760 | tf_op jit(solution)/shard_map/pallas_call | solution.py:92
  18.3 1.5 %copy-done.5 = bf16[2,1024,576]{2,1,0:T(8,128)(2,1)} copy-done((bf16[2,1024,576]{2,1,0:T(8,128)(2,1)}, bf16[2,1024,576]{2,1,0:T(8,128)(2,1)S(1)}, u32[]{:S(2)}) %copy-start.5) | copy-done | bytes 2359320
  19.8 0.1 slice.3
  19.9 1.2 %copy-done.3 = bf16[2,2,2,192,512]{4,3,2,1,0:T(8,128)(2,1)} copy-done((bf16[2,2,2,192,512]{4,3,2,1,0:T(8,128)(2,1)}, bf16[2,2,2,192,512]{4,3,2,1,0:T(8,128)(2,1)S(1)}, u32[]{:S(2)}) %copy-start.3) | copy-done | bytes 1572888
  21.0 0.1 dynamic-slice_bitcast_fusion
  21.1 0.0 copy-start.9
  21.1 4.1 %bitcast_convert_fusion = bf16[4,48,9,192]{3,1,2,0:T(8,128)(2,1)} fusion(bf16[4,48,2,512,1]{3,1,2,4,0:T(8,128)(2,1)S(1)} %bitcast.64, bf16[9,192,2,512]{3,2,1,0:T(2,128)(2,1)} %param.8), kind=kOutput, calls=%fused_computation.6 | convolution fusion | flops 679809024 | bytes 4595712 | tf_op jit(solution)/shard_map/crlow,kirw->cloki/dot_general | solution.py:413
  25.3 0.4 collective-permute-start
  25.7 0.9 %copy.15 = bf16[384,9,192]{2,0,1:T(8,128)(2,1)S(1)} copy(bf16[384,9,192]{0,2,1:T(8,128)(2,1)S(1)} %copy-done.9) | data formatting | bytes 2654208 | tf_op args[2]
  26.6 0.1 compare_select_fusion.target
  26.7 3.3 %fusion.6 = f32[4,48,9,192]{3,1,2,0:T(8,128)S(1)} fusion(bf16[4,48,2,512,1]{3,1,2,4,0:T(8,128)(2,1)S(1)} %bitcast.63, bf16[9,192,2,512]{3,2,1,0:T(2,128)(2,1)} %param.8), kind=kOutput, calls=%fused_computation.7 | convolution fusion | flops 679477248 | bytes 5259264 | tf_op jit(solution)/shard_map/crlow,kirw->cloki/dot_general | solution.py:413
  30.0 2.8 %fusion.13 = (bf16[48,9,192]{2,0,1:T(8,128)(2,1)}, bf16[48,9,192]{2,0,1:T(8,128)(2,1)}, bf16[48,9,192]{2,0,1:T(8,128)(2,1)}) fusion(f32[4,48,9,192]{3,1,2,0:T(8,128)S(1)} %fusion.6, s32[]{:T(128)S(6)} %select_n.33, bf16[4,48,9,192]{3,1,2,0:T(8,128)(2,1)} %collective-permute-done, s32[]{:T(128)S(6)} %select_n.35, s32[]{:T(128)S(6)} %select_n.34), kind=kLoop, calls=%fused_computation.17 | loop fusion | flops 746496 | bytes 1990668 | tf_op jit(solution)/shard_map/convert_element_type | solution.py:432
  32.8 3.6 %collective-permute-start.3 = (bf16[48,9,192]{2,0,1:T(8,128)(2,1)}, bf16[48,9,192]{2,0,1:T(8,128)(2,1)}, u32[]{:S(2)}, u32[]{:S(2)}) collective-permute-start(bf16[48,9,192]{2,0,1:T(8,128)(2,1)} %get-tuple-element.15), channel_id=1, source_target_pairs={{0,12},{4,0},{8,4},{12,8},{1,13},{5,1},{9,5},{13,9},{2,14},{6,2},{... | collective-permute-start | bytes 497672 | tf_op jit(solution)/shard_map/ppermute | solution.py:431
  36.4 1.0 %collective-permute-start.1 = (bf16[48,9,192]{2,0,1:T(8,128)(2,1)}, bf16[48,9,192]{2,0,1:T(8,128)(2,1)}, u32[]{:S(2)}, u32[]{:S(2)}) collective-permute-start(bf16[48,9,192]{2,0,1:T(8,128)(2,1)} %get-tuple-element.14), channel_id=1, source_target_pairs={{0,4},{4,8},{8,12},{12,0},{1,5},{5,9},{9,13},{13,1},{2,6},{6,10},{... | collective-permute-start | bytes 497672 | tf_op jit(solution)/shard_map/ppermute | solution.py:431
  37.4 17.2 %shard_map.87 = (bf16[4,2,2,96,512]{4,3,2,1,0:T(8,128)(2,1)S(1)}, f32[2,2,96,512]{3,2,1,0:T(8,128)S(1)}) custom-call(s32[2,16]{1,0:T(2,128)S(1)} %compare_select_fusion.target, s32[2,16]{1,0:T(2,128)S(1)} %copy-done.7, s32[1]{0:T(128)} %bitcast.lon, bf16[2,2,2,192,512]{4,3,2,1,0:T(8,128)(2,1)S(1)} %copy-done.4, bf16[9,384,192]{2,1,0:T(8,128)(2,1)S(1)} %bitcast.60, ...), custom_call_target="tpu_custom_call" | custom-call | flops 8999999488 | bytes 10485760 | tf_op jit(solution)/shard_map/pallas_call | solution.py:366
  54.6 0.0 copy-start.1
  54.6 0.9 %copy-done.1 = f32[2,2,96,512]{3,2,1,0:T(8,128)} copy-done((f32[2,2,96,512]{3,2,1,0:T(8,128)}, f32[2,2,96,512]{3,2,1,0:T(8,128)S(1)}, u32[]{:S(2)}) %copy-start.1) | copy-done | bytes 786456
  55.5 1.1 %copy-done.2 = f32[2,2,96,512]{3,2,1,0:T(8,128)S(1)} copy-done((f32[2,2,96,512]{3,2,1,0:T(8,128)S(1)}, f32[2,2,96,512]{3,2,1,0:T(8,128)}, u32[]{:S(2)}) %copy-start.2) | copy-done | bytes 786456
  56.6 20.8 %shard_map.88 = f32[2,192,512]{2,1,0:T(8,128)S(1)} custom-call(bf16[4,2,2,96,512]{4,3,2,1,0:T(8,128)(2,1)S(1)} %get-tuple-element.8.far_hbm, f32[2,2,96,512]{3,2,1,0:T(8,128)S(1)} %copy-done.2), custom_call_target="tpu_custom_call" | custom-call | bytes 41943040 | tf_op jit(solution)/shard_map/pallas_call | solution.py:229
  77.4 1.5 %copy.22 = f32[192,2,512]{2,1,0:T(2,128)} copy(f32[192,2,512]{2,0,1:T(8,128)S(1)} %bitcast.59) | data formatting | bytes 1572864
  78.9 2.2 %fusion.12 = f32[48,9,192]{2,0,1:T(8,128)} fusion(bf16[48,9,192]{2,0,1:T(8,128)(2,1)} %collective-permute-done.3, bf16[48,9,192]{2,0,1:T(8,128)(2,1)} %collective-permute-done.2, bf16[48,9,192]{2,0,1:T(8,128)(2,1)} %collective-permute-done.1, f32[4,48,9,192]{3,1,2,0:T(8,128)} %copy-done.8, s32[]{:T(128)S(6)} %select_n.31, ...), kind=kLoop, calls=%fused_computation.10 | loop fusion | flops 663552 | bytes 1327108 | tf_op jit(solution)/shard_map/add | solution.py:431
  (23 shorter events, 0.1 us)
Async XLA Ops:
  1.7 2.3 %copy-start = (bf16[2,16,9,64,64]{4,3,2,1,0:T(8,128)(2,1)S(1)}, bf16[2,16,9,64,64]{4,3,2,1,0:T(8,128)(2,1)}, u32[]{:S(2)}) copy-start(bf16[2,16,9,64,64]{4,3,2,1,0:T(8,128)(2,1)} %q_hbm.1) | copy-start | bytes 7077892
  18.3 1.5 %copy-start.5 = (bf16[2,1024,576]{2,1,0:T(8,128)(2,1)}, bf16[2,1024,576]{2,1,0:T(8,128)(2,1)S(1)}, u32[]{:S(2)}) copy-start(bf16[2,1024,576]{2,1,0:T(8,128)(2,1)S(1)} %get-tuple-element.7.t_ref) | copy-start | bytes 7077892
  19.9 1.2 %copy-start.3 = (bf16[2,2,2,192,512]{4,3,2,1,0:T(8,128)(2,1)}, bf16[2,2,2,192,512]{4,3,2,1,0:T(8,128)(2,1)S(1)}, u32[]{:S(2)}) copy-start(bf16[2,2,2,192,512]{4,3,2,1,0:T(8,128)(2,1)S(1)} %get-tuple-element.6.g_ref) | copy-start | bytes 4718596
  21.1 4.5 %copy-start.9 = (bf16[384,9,192]{0,2,1:T(8,128)(2,1)S(1)}, bf16[384,9,192]{0,2,1:T(8,128)(2,1)}, u32[]{:S(2)}) copy-start(bf16[384,9,192]{0,2,1:T(8,128)(2,1)} %param.9) | copy-start | bytes 3981316
  25.3 1.3 %copy-start.10 = (s32[2,16]{1,0:T(2,128)S(1)}, s32[2,16]{1,0:T(2,128)}, u32[]{:S(2)}) copy-start(s32[2,16]{1,0:T(2,128)} %param.11) | copy-start | bytes 388
  25.3 1.3 %copy-start.11 = (s32[2]{0:T(128)S(1)}, s32[2]{0:T(128)}, u32[]{:S(2)}) copy-start(s32[2]{0:T(128)} %param.13) | copy-start | bytes 28
  25.3 4.7 %collective-permute-start = (bf16[4,48,9,192]{3,1,2,0:T(8,128)(2,1)}, bf16[4,48,9,192]{3,1,2,0:T(8,128)(2,1)}, u32[]{:S(2)}, u32[]{:S(2)}) collective-permute-start(bf16[4,48,9,192]{3,1,2,0:T(8,128)(2,1)} %bitcast_convert_fusion), channel_id=1, source_target_pairs={{0,1},{1,0},{2,3},{3,2},{4,5},{5,4},{6,7},{7,6},{8,9},{9,8},{10,11... | collective-permute-start | bytes 1990664 | tf_op jit(solution)/shard_map/ppermute | solution.py:421
  26.7 10.7 %copy-start.4 = (bf16[2,2,2,192,512]{4,3,2,1,0:T(8,128)(2,1)S(1)}, bf16[2,2,2,192,512]{4,3,2,1,0:T(8,128)(2,1)}, u32[]{:S(2)}) copy-start(bf16[2,2,2,192,512]{4,3,2,1,0:T(8,128)(2,1)} %copy-done.3) | copy-start | bytes 4718596
  26.7 10.7 %copy-start.6 = (bf16[2,1024,576]{2,1,0:T(8,128)(2,1)S(1)}, bf16[2,1024,576]{2,1,0:T(8,128)(2,1)}, u32[]{:S(2)}) copy-start(bf16[2,1024,576]{2,1,0:T(8,128)(2,1)} %copy-done.5) | copy-start | bytes 7077892
  26.7 10.7 %copy-start.7 = (s32[2,16]{1,0:T(2,128)S(1)}, s32[2,16]{1,0:T(2,128)}, u32[]{:S(2)}) copy-start(s32[2,16]{1,0:T(2,128)} %shift.1) | copy-start | bytes 388
  30.0 7.4 %copy-start.8 = (f32[4,48,9,192]{3,1,2,0:T(8,128)}, f32[4,48,9,192]{3,1,2,0:T(8,128)S(1)}, u32[]{:S(2)}) copy-start(f32[4,48,9,192]{3,1,2,0:T(8,128)S(1)} %fusion.6) | copy-start | bytes 3981316
  32.8 46.2 %collective-permute-start.3 = (bf16[48,9,192]{2,0,1:T(8,128)(2,1)}, bf16[48,9,192]{2,0,1:T(8,128)(2,1)}, u32[]{:S(2)}, u32[]{:S(2)}) collective-permute-start(bf16[48,9,192]{2,0,1:T(8,128)(2,1)} %get-tuple-element.15), channel_id=1, source_target_pairs={{0,12},{4,0},{8,4},{12,8},{1,13},{5,1},{9,5},{13,9},{2,14},{6,2},{... | collective-permute-start | bytes 497672 | tf_op jit(solution)/shard_map/ppermute | solution.py:431
  36.4 42.5 %collective-permute-start.2 = (bf16[48,9,192]{2,0,1:T(8,128)(2,1)}, bf16[48,9,192]{2,0,1:T(8,128)(2,1)}, u32[]{:S(2)}, u32[]{:S(2)}) collective-permute-start(bf16[48,9,192]{2,0,1:T(8,128)(2,1)} %get-tuple-element.16), channel_id=1, source_target_pairs={{0,8},{4,12},{8,0},{12,4},{1,9},{5,13},{9,1},{13,5},{2,10},{6,14},... | collective-permute-start | bytes 497672 | tf_op jit(solution)/shard_map/ppermute | solution.py:431
  36.4 42.5 %collective-permute-start.1 = (bf16[48,9,192]{2,0,1:T(8,128)(2,1)}, bf16[48,9,192]{2,0,1:T(8,128)(2,1)}, u32[]{:S(2)}, u32[]{:S(2)}) collective-permute-start(bf16[48,9,192]{2,0,1:T(8,128)(2,1)} %get-tuple-element.14), channel_id=1, source_target_pairs={{0,4},{4,8},{8,12},{12,0},{1,5},{5,9},{9,13},{13,1},{2,6},{6,10},{... | collective-permute-start | bytes 497672 | tf_op jit(solution)/shard_map/ppermute | solution.py:431
  54.6 0.9 %copy-start.1 = (f32[2,2,96,512]{3,2,1,0:T(8,128)}, f32[2,2,96,512]{3,2,1,0:T(8,128)S(1)}, u32[]{:S(2)}) copy-start(f32[2,2,96,512]{3,2,1,0:T(8,128)S(1)} %get-tuple-element.9.near_hbm) | copy-start | bytes 2359300
  55.5 1.1 %copy-start.2 = (f32[2,2,96,512]{3,2,1,0:T(8,128)S(1)}, f32[2,2,96,512]{3,2,1,0:T(8,128)}, u32[]{:S(2)}) copy-start(f32[2,2,96,512]{3,2,1,0:T(8,128)} %copy-done.1) | copy-start | bytes 2359300

commit v5 on v4

--- a/solution.py
+++ b/solution.py
@@ -104,7 +104,7 @@
             pltpu.SemaphoreType.DMA((2 * groups, rows)),
         ],
         compiler_params=pltpu.CompilerParams(
-            collective_id=0, has_side_effects=True, vmem_limit_bytes=20 * MIB
+            collective_id=0, has_side_effects=True, vmem_limit_bytes=48 * MIB
         ),
         cost_estimate=pl.CostEstimate(flops=0, bytes_accessed=10 * 2**20, transcendentals=0),
     )(turned_out, quad_tiles)

time: 81.4 us -> 78.8 us (0.968)
  local copies, waits for them, and re-layouts: 10.6 us -> 8.28 us
    unnamed x27 -> x25, local copies, waits for them, and re-layouts: 10.4 us -> 8.11 us
  transfers between devices with their start and end apart: 4 -> 4, of which waited for: 0 -> 0; matrix products, arithmetic and copies ran while one was open for 7% -> 7% of each run, Pallas kernels for 47% -> 48%
where the time goes in v5:
time: 78.8 us; the launch traced here: 78.5 us
  Pallas kernels  52 us (66%)
  local copies, waits for them, and re-layouts  8.28 us (11%)
  matrix products  7.41 us (9%)
  other arithmetic  5.02 us (6%)
  starting transfers between devices  4.98 us (6%)
  between operations  0.8 us (1%)
    pallas_call x1, Pallas kernels, summed(): pl.pallas_call(sum_kernel, out_shape=jax.ShapeDtypeStruct((rows, 2 * own_...  20.8 us
    pallas_call x1, Pallas kernels, quadrature(): pl.pallas_call(functools.partial(quadrature_kernel, own_half), out_shape=...  17.2 us
    pallas_call x1, Pallas kernels, gathered(): pl.pallas_call(gather_kernel, out_shape=(jax.ShapeDtypeStruct((2, groups,...  14 us
    unnamed x25, local copies, waits for them, and re-layouts  8.11 us
    dot_general x2, matrix products, half(): jnp.einsum('crlow,kirw->cloki', lax.dynamic_index_in_dim(split, which, 3,...  7.41 us
    ppermute x3, starting transfers between devices, filter_gradient(): lax.ppermute(both(step).astype(jnp.bfloat16), 'lat', [(at, (at + step) %...  4.61 us
    convert_element_type x1, other arithmetic, filter_gradient(): both(step).astype(jnp.bfloat16)  2.75 us
    add x1, other arithmetic, filter_gradient(): result + lax.ppermute(both(step).astype(jnp.bfloat16), 'lat', [(at, (at +...  2.21 us
  transfers between devices with their start and end apart: 4, of which 0 were waited for; matrix products, arithmetic and copies ran while one was open for 7% of the time, Pallas kernels for 48%

profile of v5, /device:TPU:0, one launch (start us, length us, event | category | flops | bytes accessed | tf_op | source)
XLA Modules:
  0.0 78.5 jit_solution(1831285308203984049)
XLA Ops:
  0.6 1.0 %copy.42 = bf16[192,2,512]{2,0,1:T(8,128)(2,1)S(1)} copy(bf16[192,2,512]{2,1,0:T(2,128)(2,1)} %param.7) | data formatting | bytes 786432 | tf_op args[0]
  1.7 14.0 %shard_map.86 = (bf16[2,2,2,192,512]{4,3,2,1,0:T(8,128)(2,1)S(1)}, bf16[2,1024,576]{2,1,0:T(8,128)(2,1)S(1)}) custom-call(bf16[2,192,512]{2,1,0:T(8,128)(2,1)S(1)} %bitcast.61, bf16[2,16,9,64,64]{4,3,2,1,0:T(8,128)(2,1)} %q_hbm.1), custom_call_target="tpu_custom_call" | custom-call | bytes 10485760 | tf_op jit(solution)/shard_map/pallas_call | solution.py:92
  15.7 1.5 %copy-done.4 = bf16[2,1024,576]{2,1,0:T(8,128)(2,1)} copy-done((bf16[2,1024,576]{2,1,0:T(8,128)(2,1)}, bf16[2,1024,576]{2,1,0:T(8,128)(2,1)S(1)}, u32[]{:S(2)}) %copy-start.4) | copy-done | bytes 2359320
  17.2 0.1 slice.3
  17.2 1.2 %copy-done.2 = bf16[2,2,2,192,512]{4,3,2,1,0:T(8,128)(2,1)} copy-done((bf16[2,2,2,192,512]{4,3,2,1,0:T(8,128)(2,1)}, bf16[2,2,2,192,512]{4,3,2,1,0:T(8,128)(2,1)S(1)}, u32[]{:S(2)}) %copy-start.2) | copy-done | bytes 1572888
  18.4 0.1 dynamic-slice_bitcast_fusion
  18.5 0.0 copy-start.8
  18.5 4.2 %bitcast_convert_fusion = bf16[4,48,9,192]{3,1,2,0:T(8,128)(2,1)} fusion(bf16[4,48,2,512,1]{3,1,2,4,0:T(8,128)(2,1)S(1)} %bitcast.64, bf16[9,192,2,512]{3,2,1,0:T(2,128)(2,1)} %param.8), kind=kOutput, calls=%fused_computation.6 | convolution fusion | flops 679809024 | bytes 4595712 | tf_op jit(solution)/shard_map/crlow,kirw->cloki/dot_general | solution.py:413
  22.7 0.4 collective-permute-start
  23.1 0.9 %copy.15 = bf16[384,9,192]{2,0,1:T(8,128)(2,1)S(1)} copy(bf16[384,9,192]{0,2,1:T(8,128)(2,1)S(1)} %copy-done.8) | data formatting | bytes 2654208 | tf_op args[2]
  24.0 0.1 compare_select_fusion.target
  24.1 3.3 %fusion.6 = f32[4,48,9,192]{3,1,2,0:T(8,128)S(1)} fusion(bf16[4,48,2,512,1]{3,1,2,4,0:T(8,128)(2,1)S(1)} %bitcast.63, bf16[9,192,2,512]{3,2,1,0:T(2,128)(2,1)} %param.8), kind=kOutput, calls=%fused_computation.7 | convolution fusion | flops 679477248 | bytes 5259264 | tf_op jit(solution)/shard_map/crlow,kirw->cloki/dot_general | solution.py:413
  27.4 0.0 collective-permute-done
  27.4 2.7 %fusion.13 = (bf16[48,9,192]{2,0,1:T(8,128)(2,1)}, bf16[48,9,192]{2,0,1:T(8,128)(2,1)}, bf16[48,9,192]{2,0,1:T(8,128)(2,1)}) fusion(f32[4,48,9,192]{3,1,2,0:T(8,128)S(1)} %fusion.6, s32[]{:T(128)S(6)} %select_n.33, bf16[4,48,9,192]{3,1,2,0:T(8,128)(2,1)} %collective-permute-done, s32[]{:T(128)S(6)} %select_n.35, s32[]{:T(128)S(6)} %select_n.34), kind=kLoop, calls=%fused_computation.17 | loop fusion | flops 746496 | bytes 1990668 | tf_op jit(solution)/shard_map/convert_element_type | solution.py:432
  30.1 3.6 %collective-permute-start.3 = (bf16[48,9,192]{2,0,1:T(8,128)(2,1)}, bf16[48,9,192]{2,0,1:T(8,128)(2,1)}, u32[]{:S(2)}, u32[]{:S(2)}) collective-permute-start(bf16[48,9,192]{2,0,1:T(8,128)(2,1)} %get-tuple-element.15), channel_id=1, source_target_pairs={{0,12},{4,0},{8,4},{12,8},{1,13},{5,1},{9,5},{13,9},{2,14},{6,2},{... | collective-permute-start | bytes 497672 | tf_op jit(solution)/shard_map/ppermute | solution.py:431
  33.7 1.0 %collective-permute-start.1 = (bf16[48,9,192]{2,0,1:T(8,128)(2,1)}, bf16[48,9,192]{2,0,1:T(8,128)(2,1)}, u32[]{:S(2)}, u32[]{:S(2)}) collective-permute-start(bf16[48,9,192]{2,0,1:T(8,128)(2,1)} %get-tuple-element.14), channel_id=1, source_target_pairs={{0,4},{4,8},{8,12},{12,0},{1,5},{5,9},{9,13},{13,1},{2,6},{6,10},{... | collective-permute-start | bytes 497672 | tf_op jit(solution)/shard_map/ppermute | solution.py:431
  34.8 17.2 %shard_map.87 = (bf16[4,2,2,96,512]{4,3,2,1,0:T(8,128)(2,1)S(1)}, f32[2,2,96,512]{3,2,1,0:T(8,128)S(1)}) custom-call(s32[2,16]{1,0:T(2,128)S(1)} %compare_select_fusion.target, s32[2,16]{1,0:T(2,128)S(1)} %copy-done.6, s32[1]{0:T(128)} %bitcast.lon, bf16[2,2,2,192,512]{4,3,2,1,0:T(8,128)(2,1)S(1)} %copy-done.3, bf16[9,384,192]{2,1,0:T(8,128)(2,1)S(1)} %bitcast.60, ...), custom_call_target="tpu_custom_call" | custom-call | flops 8999999488 | bytes 10485760 | tf_op jit(solution)/shard_map/pallas_call | solution.py:366
  52.0 0.0 copy-start
  52.0 0.9 %copy-done = f32[2,2,96,512]{3,2,1,0:T(8,128)} copy-done((f32[2,2,96,512]{3,2,1,0:T(8,128)}, f32[2,2,96,512]{3,2,1,0:T(8,128)S(1)}, u32[]{:S(2)}) %copy-start) | copy-done | bytes 786456
  52.8 1.1 %copy-done.1 = f32[2,2,96,512]{3,2,1,0:T(8,128)S(1)} copy-done((f32[2,2,96,512]{3,2,1,0:T(8,128)S(1)}, f32[2,2,96,512]{3,2,1,0:T(8,128)}, u32[]{:S(2)}) %copy-start.1) | copy-done | bytes 786456
  54.0 20.8 %shard_map.88 = f32[2,192,512]{2,1,0:T(8,128)S(1)} custom-call(bf16[4,2,2,96,512]{4,3,2,1,0:T(8,128)(2,1)S(1)} %get-tuple-element.8.far_hbm, f32[2,2,96,512]{3,2,1,0:T(8,128)S(1)} %copy-done.1), custom_call_target="tpu_custom_call" | custom-call | bytes 41943040 | tf_op jit(solution)/shard_map/pallas_call | solution.py:229
  74.8 1.5 %copy.22 = f32[192,2,512]{2,1,0:T(2,128)} copy(f32[192,2,512]{2,0,1:T(8,128)S(1)} %bitcast.59) | data formatting | bytes 1572864
  76.3 0.0 collective-permute-done.3
  76.3 2.2 %fusion.12 = f32[48,9,192]{2,0,1:T(8,128)} fusion(bf16[48,9,192]{2,0,1:T(8,128)(2,1)} %collective-permute-done.3, bf16[48,9,192]{2,0,1:T(8,128)(2,1)} %collective-permute-done.2, bf16[48,9,192]{2,0,1:T(8,128)(2,1)} %collective-permute-done.1, f32[4,48,9,192]{3,1,2,0:T(8,128)} %copy-done.7, s32[]{:T(128)S(6)} %select_n.31, ...), kind=kLoop, calls=%fused_computation.10 | loop fusion | flops 663552 | bytes 1327108 | tf_op jit(solution)/shard_map/add | solution.py:431
  (21 shorter events, 0.1 us)
Async XLA Ops:
  15.7 1.5 %copy-start.4 = (bf16[2,1024,576]{2,1,0:T(8,128)(2,1)}, bf16[2,1024,576]{2,1,0:T(8,128)(2,1)S(1)}, u32[]{:S(2)}) copy-start(bf16[2,1024,576]{2,1,0:T(8,128)(2,1)S(1)} %get-tuple-element.7.t_ref) | copy-start | bytes 7077892
  17.2 1.2 %copy-start.2 = (bf16[2,2,2,192,512]{4,3,2,1,0:T(8,128)(2,1)}, bf16[2,2,2,192,512]{4,3,2,1,0:T(8,128)(2,1)S(1)}, u32[]{:S(2)}) copy-start(bf16[2,2,2,192,512]{4,3,2,1,0:T(8,128)(2,1)S(1)} %get-tuple-element.6.g_ref) | copy-start | bytes 4718596
  18.5 4.5 %copy-start.8 = (bf16[384,9,192]{0,2,1:T(8,128)(2,1)S(1)}, bf16[384,9,192]{0,2,1:T(8,128)(2,1)}, u32[]{:S(2)}) copy-start(bf16[384,9,192]{0,2,1:T(8,128)(2,1)} %param.9) | copy-start | bytes 3981316
  22.7 1.3 %copy-start.9 = (s32[2,16]{1,0:T(2,128)S(1)}, s32[2,16]{1,0:T(2,128)}, u32[]{:S(2)}) copy-start(s32[2,16]{1,0:T(2,128)} %param.11) | copy-start | bytes 388
  22.7 1.3 %copy-start.10 = (s32[2]{0:T(128)S(1)}, s32[2]{0:T(128)}, u32[]{:S(2)}) copy-start(s32[2]{0:T(128)} %param.13) | copy-start | bytes 28
  22.7 4.7 %collective-permute-start = (bf16[4,48,9,192]{3,1,2,0:T(8,128)(2,1)}, bf16[4,48,9,192]{3,1,2,0:T(8,128)(2,1)}, u32[]{:S(2)}, u32[]{:S(2)}) collective-permute-start(bf16[4,48,9,192]{3,1,2,0:T(8,128)(2,1)} %bitcast_convert_fusion), channel_id=1, source_target_pairs={{0,1},{1,0},{2,3},{3,2},{4,5},{5,4},{6,7},{7,6},{8,9},{9,8},{10,11... | collective-permute-start | bytes 1990664 | tf_op jit(solution)/shard_map/ppermute | solution.py:421
  24.1 10.7 %copy-start.3 = (bf16[2,2,2,192,512]{4,3,2,1,0:T(8,128)(2,1)S(1)}, bf16[2,2,2,192,512]{4,3,2,1,0:T(8,128)(2,1)}, u32[]{:S(2)}) copy-start(bf16[2,2,2,192,512]{4,3,2,1,0:T(8,128)(2,1)} %copy-done.2) | copy-start | bytes 4718596
  24.1 10.7 %copy-start.5 = (bf16[2,1024,576]{2,1,0:T(8,128)(2,1)S(1)}, bf16[2,1024,576]{2,1,0:T(8,128)(2,1)}, u32[]{:S(2)}) copy-start(bf16[2,1024,576]{2,1,0:T(8,128)(2,1)} %copy-done.4) | copy-start | bytes 7077892
  24.1 10.7 %copy-start.6 = (s32[2,16]{1,0:T(2,128)S(1)}, s32[2,16]{1,0:T(2,128)}, u32[]{:S(2)}) copy-start(s32[2,16]{1,0:T(2,128)} %shift.1) | copy-start | bytes 388
  27.4 7.4 %copy-start.7 = (f32[4,48,9,192]{3,1,2,0:T(8,128)}, f32[4,48,9,192]{3,1,2,0:T(8,128)S(1)}, u32[]{:S(2)}) copy-start(f32[4,48,9,192]{3,1,2,0:T(8,128)S(1)} %fusion.6) | copy-start | bytes 3981316
  30.1 46.1 %collective-permute-start.3 = (bf16[48,9,192]{2,0,1:T(8,128)(2,1)}, bf16[48,9,192]{2,0,1:T(8,128)(2,1)}, u32[]{:S(2)}, u32[]{:S(2)}) collective-permute-start(bf16[48,9,192]{2,0,1:T(8,128)(2,1)} %get-tuple-element.15), channel_id=1, source_target_pairs={{0,12},{4,0},{8,4},{12,8},{1,13},{5,1},{9,5},{13,9},{2,14},{6,2},{... | collective-permute-start | bytes 497672 | tf_op jit(solution)/shard_map/ppermute | solution.py:431
  33.7 42.5 %collective-permute-start.2 = (bf16[48,9,192]{2,0,1:T(8,128)(2,1)}, bf16[48,9,192]{2,0,1:T(8,128)(2,1)}, u32[]{:S(2)}, u32[]{:S(2)}) collective-permute-start(bf16[48,9,192]{2,0,1:T(8,128)(2,1)} %get-tuple-element.16), channel_id=1, source_target_pairs={{0,8},{4,12},{8,0},{12,4},{1,9},{5,13},{9,1},{13,5},{2,10},{6,14},... | collective-permute-start | bytes 497672 | tf_op jit(solution)/shard_map/ppermute | solution.py:431
  33.7 42.5 %collective-permute-start.1 = (bf16[48,9,192]{2,0,1:T(8,128)(2,1)}, bf16[48,9,192]{2,0,1:T(8,128)(2,1)}, u32[]{:S(2)}, u32[]{:S(2)}) collective-permute-start(bf16[48,9,192]{2,0,1:T(8,128)(2,1)} %get-tuple-element.14), channel_id=1, source_target_pairs={{0,4},{4,8},{8,12},{12,0},{1,5},{5,9},{9,13},{13,1},{2,6},{6,10},{... | collective-permute-start | bytes 497672 | tf_op jit(solution)/shard_map/ppermute | solution.py:431
  52.0 0.9 %copy-start = (f32[2,2,96,512]{3,2,1,0:T(8,128)}, f32[2,2,96,512]{3,2,1,0:T(8,128)S(1)}, u32[]{:S(2)}) copy-start(f32[2,2,96,512]{3,2,1,0:T(8,128)S(1)} %get-tuple-element.9.near_hbm) | copy-start | bytes 2359300
  52.8 1.1 %copy-start.1 = (f32[2,2,96,512]{3,2,1,0:T(8,128)S(1)}, f32[2,2,96,512]{3,2,1,0:T(8,128)}, u32[]{:S(2)}) copy-start(f32[2,2,96,512]{3,2,1,0:T(8,128)} %copy-done) | copy-start | bytes 2359300
